TPU v7x, 32 devices: a whole 2x2x4 slice. The times are simulated.
32 devices in a mesh: tower: 2 (over core), rows: 16 (over z, y, x).
Axes of the slice: x: 2, y: 2, z: 4, core: 2. Of those that a mesh axis runs over, the one named last changes fastest.
Arguments:
- tokens: bfloat16 [2, 4096, 768], P('tower', 'rows'), may hold values from -6 to 6
- query_segments: int32 [16, 256], P('rows'), may hold values from 0 to 3, never falling along the last dimension, each value on 1 to 96 neighbouring positions
- doc_lengths: int32 [16], P('rows'), may hold values from 1 to 256, 2560 in all
- bucket_table: int32 [511], replicated, may hold values from 0 to 31, as said below
- positives: int32 [16, 4], replicated, may hold values from 0 to 15
- gain_attn: float32 [768], replicated, may hold values from 0.1 to 1.9
- w_query_key: bfloat16 [768, 1536], replicated, may hold values from -0.109375 to 0.109375
- w_value: bfloat16 [768, 768], replicated, may hold values from -0.21875 to 0.21875
- w_attn_out: bfloat16 [768, 768], replicated, may hold values from -0.625 to 0.625
- rel_bias: float32 [32, 12], replicated, may hold values from -4 to 4
- gain_ff: float32 [768], replicated, may hold values from 0.1 to 1.9
- w_in: bfloat16 [768, 3072], replicated, may hold values from -0.21875 to 0.21875
- w_out: bfloat16 [3072, 768], replicated, may hold values from -0.1875 to 0.1875
- gain_final: float32 [768], replicated, may hold values from 0.1 to 1.9
- w_proj: bfloat16 [768, 768], replicated, may hold values from -0.21875 to 0.21875
Outputs:
- loss: float32 [], replicated
- tokens_grad: float32 [2, 4096, 768], P('tower', 'rows')
- gain_attn_grad: float32 [768], replicated
- w_query_key_grad: float32 [768, 1536], P('rows', 'tower')
- w_value_grad: float32 [768, 768], P('rows', 'tower')
- w_attn_out_grad: float32 [768, 768], P('rows', 'tower')
- rel_bias_grad: float32 [32, 12], replicated
- gain_ff_grad: float32 [768], replicated
- w_in_grad: float32 [768, 3072], P('rows', 'tower')
- w_out_grad: float32 [3072, 768], P('rows', 'tower')
- gain_final_grad: float32 [768], replicated
- w_proj_grad: float32 [768, 768], P('rows', 'tower')
Inputs may be any that keep to these rules, and one draw needn't show every extreme that they name: `query_segments`: each row's ids do not fall; each of the 4 ids names 1 to 96 slots of the row, one exactly 96. `doc_lengths`: one document has exactly 256 tokens. `bucket_table`: entry m holds the bucket of the offset m - (255) of key position minus query position: magnitudes under 8 have their own buckets 0 to 7, larger magnitudes buckets 8 to 15 not falling with the magnitude; positive offsets add 16.
All inputs are finite; a program needn't handle non-finite values. No bound on the sum of `doc_lengths` on one device may be relied on, other than what follows from the above.
Results may differ from a plain program's by a relative error of at most 0.018.
Values may be sent and summed in bfloat16 or wider, within the bound.
A program may use at most 192 MiB of HBM per device.

v0:
```python
import jax
import jax.numpy as jnp
from jax import lax
from jax.sharding import PartitionSpec as P

EPSILON = 1e-06
LOGIT_SCALE = 50.0
MASKED = -1000000000.0
HIGHEST = lax.Precision.HIGHEST


def norm_forward(values, gain):
    inverse = lax.rsqrt(jnp.mean(values * values, axis=-1, keepdims=True) + EPSILON)
    return (values * inverse * gain, inverse)


def norm_backward(values, inverse, gain, upstream):
    scaled = upstream * gain
    gain_grad = jnp.sum(upstream * values * inverse, axis=0)
    inner = jnp.mean(scaled * values, axis=-1, keepdims=True)
    return (inverse * scaled - values * inverse * inverse * inverse * inner, gain_grad)


def block_scores(query_heads, key_heads, segment, table_rows, start, count):
    width = key_heads.shape[0]
    raw = jnp.einsum("ihd,jhd->hij", query_heads, key_heads, preferred_element_type=jnp.float32)
    offsets = jnp.arange(width)[None, :] - (start + jnp.arange(count))[:, None] + width - 1
    biased = raw + jnp.take(table_rows, offsets, axis=1)
    allowed = segment[start : start + count, None] == segment[None, :]
    return (jnp.where(allowed[None], biased, MASKED), offsets)


def on_device(
    tokens,
    query_segments,
    doc_lengths,
    bucket_table,
    positives,
    gain_attn,
    w_query_key,
    w_value,
    w_attn_out,
    rel_bias,
    gain_ff,
    w_in,
    w_out,
    gain_final,
    w_proj,
):
    is_query = lax.axis_index("tower") == 0
    row_index = lax.axis_index("rows")
    query_flag = jnp.where(is_query, 1.0, 0.0).astype(jnp.float32)
    inputs = tokens[0].astype(jnp.float32)
    width, model = inputs.shape
    heads = rel_bias.shape[1]
    buckets = rel_bias.shape[0]
    head_size = model // heads
    positions = jnp.arange(width)
    doc_segment = jnp.where(positions < doc_lengths[0], 0, 1).astype(jnp.int32)
    segment = jnp.where(is_query, query_segments[0], doc_segment)
    queries = positives.shape[1]
    member = (segment[None, :] == jnp.arange(queries)[:, None]).astype(jnp.float32)
    pool = member / jnp.maximum(jnp.sum(member, axis=-1, keepdims=True), 1.0)
    bucket_hot = (bucket_table[:, None] == jnp.arange(buckets)[None, :]).astype(jnp.float32)
    table_rows = jnp.einsum("mb,bh->hm", bucket_hot, rel_bias, precision=HIGHEST)
    normed, inverse_one = norm_forward(inputs, gain_attn)
    normed_low = normed.astype(jnp.bfloat16)
    query_key = jnp.dot(normed_low, w_query_key, preferred_element_type=jnp.float32).astype(
        jnp.bfloat16
    )
    values_low = jnp.dot(normed_low, w_value, preferred_element_type=jnp.float32).astype(
        jnp.bfloat16
    )
    query_heads = query_key[:, :model].reshape(width, heads, head_size)
    key_heads = query_key[:, model:].reshape(width, heads, head_size)
    value_heads = values_low.reshape(width, heads, head_size)
    block = min(512, width)
    start = 0
    scores, unused = block_scores(query_heads, key_heads, segment, table_rows, start, block)
    highest = jnp.max(scores, axis=-1, keepdims=True)
    weights = jnp.exp(scores - highest)
    summed = jnp.sum(weights, axis=-1, keepdims=True)
    probs_low = (weights / summed).astype(jnp.bfloat16)
    total_parts = highest + jnp.log(summed)
    mixed_parts = jnp.einsum(
        "hij,jhd->ihd", probs_low, value_heads, preferred_element_type=jnp.float32
    )
    mixed_low = mixed_parts.reshape(width, model).astype(jnp.bfloat16)
    hidden_one = inputs + jnp.dot(mixed_low, w_attn_out, preferred_element_type=jnp.float32)
    normed_two, inverse_two = norm_forward(hidden_one, gain_ff)
    normed_two_low = normed_two.astype(jnp.bfloat16)
    inner = jnp.dot(normed_two_low, w_in, preferred_element_type=jnp.float32)
    active, gelu_back = jax.vjp(lambda value: jax.nn.gelu(value, approximate=True), inner)
    active_low = active.astype(jnp.bfloat16)
    hidden_two = hidden_one + jnp.dot(active_low, w_out, preferred_element_type=jnp.float32)
    normed_three, inverse_three = norm_forward(hidden_two, gain_final)
    pooled_low = jnp.dot(
        pool, normed_three, precision=HIGHEST, preferred_element_type=jnp.float32
    ).astype(jnp.bfloat16)
    projected = jnp.dot(pooled_low, w_proj, preferred_element_type=jnp.float32)
    length_inverse = lax.rsqrt(jnp.sum(projected * projected, axis=-1, keepdims=True) + EPSILON)
    embed_low = (projected * length_inverse).astype(jnp.bfloat16)
    gathered = lax.all_gather(embed_low, ("tower", "rows"), axis=0, tiled=True)
    half_count = gathered.shape[0] // 2
    row_count = half_count // queries
    query_low = gathered[:half_count]
    doc_low = gathered[half_count:].reshape(row_count, queries, model)[:, 0]
    doc_embeds = doc_low.astype(jnp.float32)
    query_embeds = query_low.astype(jnp.float32)
    logits = LOGIT_SCALE * jnp.dot(query_low, doc_low.T, preferred_element_type=jnp.float32)
    highest_logit = jnp.max(logits, axis=-1, keepdims=True)
    log_sum = highest_logit + jnp.log(
        jnp.sum(jnp.exp(logits - highest_logit), axis=-1, keepdims=True)
    )
    target = (positives.reshape(-1)[:, None] == jnp.arange(row_count)[None, :]).astype(jnp.float32)
    total_queries = row_count * queries
    dlogits = (jnp.exp(logits - log_sum) - target) * (LOGIT_SCALE / total_queries)
    first_query = row_index * queries
    own_sum = lax.dynamic_slice_in_dim(log_sum, first_query, queries, 0)
    own_logits = lax.dynamic_slice_in_dim(logits, first_query, queries, 0)
    own_target = lax.dynamic_slice_in_dim(target, first_query, queries, 0)
    picked = jnp.sum(own_logits * own_target, axis=-1, keepdims=True)
    local_loss = jnp.sum(own_sum - picked) * query_flag
    own_dlogits = lax.dynamic_slice_in_dim(dlogits, first_query, queries, 0)
    query_grad_rows = jnp.dot(
        own_dlogits, doc_embeds, precision=HIGHEST, preferred_element_type=jnp.float32
    )
    column = lax.dynamic_slice_in_dim(dlogits, row_index, 1, 1)
    doc_grad = jnp.dot(
        column.T, query_embeds, precision=HIGHEST, preferred_element_type=jnp.float32
    )
    doc_rows = jnp.concatenate([doc_grad, jnp.zeros((queries - 1, model), jnp.float32)], axis=0)
    embed_grad = jnp.where(is_query, query_grad_rows, doc_rows)
    along = jnp.sum(embed_grad * projected, axis=-1, keepdims=True)
    proj_grad = (
        length_inverse * embed_grad
        - projected * length_inverse * length_inverse * length_inverse * along
    )
    proj_grad_low = proj_grad.astype(jnp.bfloat16)
    w_proj_grad = jnp.einsum(
        "qi,qd->id", pooled_low, proj_grad_low, preferred_element_type=jnp.float32
    )
    pooled_grad = jnp.einsum("qd,id->qi", proj_grad_low, w_proj, preferred_element_type=jnp.float32)
    normed_three_grad = jnp.dot(
        pool.T, pooled_grad, precision=HIGHEST, preferred_element_type=jnp.float32
    )
    hidden_two_grad, gain_final_grad = norm_backward(
        hidden_two, inverse_three, gain_final, normed_three_grad
    )
    branch_low = hidden_two_grad.astype(jnp.bfloat16)
    w_out_grad = jnp.einsum("tf,td->fd", active_low, branch_low, preferred_element_type=jnp.float32)
    active_grad = jnp.einsum("td,fd->tf", branch_low, w_out, preferred_element_type=jnp.float32)
    inner_low = gelu_back(active_grad)[0].astype(jnp.bfloat16)
    w_in_grad = jnp.einsum(
        "td,tf->df", normed_two_low, inner_low, preferred_element_type=jnp.float32
    )
    normed_two_grad = jnp.einsum("tf,df->td", inner_low, w_in, preferred_element_type=jnp.float32)
    through_two, gain_ff_grad = norm_backward(hidden_one, inverse_two, gain_ff, normed_two_grad)
    hidden_one_grad = hidden_two_grad + through_two
    attn_low = hidden_one_grad.astype(jnp.bfloat16)
    w_attn_out_grad = jnp.einsum(
        "ti,td->id", mixed_low, attn_low, preferred_element_type=jnp.float32
    )
    mixed_grad_low = jnp.einsum(
        "td,id->ti", attn_low, w_attn_out, preferred_element_type=jnp.float32
    ).astype(jnp.bfloat16)
    mixed_grad_heads = mixed_grad_low.reshape(width, heads, head_size)
    start = 0
    scores, offsets = block_scores(query_heads, key_heads, segment, table_rows, start, block)
    probs = jnp.exp(scores - total_parts)
    probs_grad = jnp.einsum(
        "ihd,jhd->hij", mixed_grad_heads, value_heads, preferred_element_type=jnp.float32
    )
    score_grad = probs * (probs_grad - jnp.sum(probs * probs_grad, axis=-1, keepdims=True))
    pair_bucket = jnp.take(bucket_table, offsets.reshape(-1))
    pair_hot = (pair_bucket[:, None] == jnp.arange(buckets)[None, :]).astype(jnp.bfloat16)
    flat_grad = score_grad.reshape(heads, -1)
    upper_part = flat_grad.astype(jnp.bfloat16)
    lower_part = (flat_grad - upper_part.astype(jnp.float32)).astype(jnp.bfloat16)
    bias_grad = jnp.dot(upper_part, pair_hot, preferred_element_type=jnp.float32)
    bias_grad = bias_grad + jnp.dot(lower_part, pair_hot, preferred_element_type=jnp.float32)
    score_low = score_grad.astype(jnp.bfloat16)
    query_parts = jnp.einsum(
        "hij,jhd->ihd", score_low, key_heads, preferred_element_type=jnp.float32
    )
    key_grad = jnp.einsum(
        "hij,ihd->jhd", score_low, query_heads, preferred_element_type=jnp.float32
    )
    value_grad = jnp.einsum(
        "hij,ihd->jhd",
        probs.astype(jnp.bfloat16),
        mixed_grad_heads,
        preferred_element_type=jnp.float32,
    )
    both_low = jnp.concatenate(
        [query_parts.reshape(width, model), key_grad.reshape(width, model)], axis=1
    ).astype(jnp.bfloat16)
    value_low = value_grad.reshape(width, model).astype(jnp.bfloat16)
    w_query_key_grad = jnp.einsum(
        "td,tk->dk", normed_low, both_low, preferred_element_type=jnp.float32
    )
    w_value_grad = jnp.einsum(
        "td,tk->dk", normed_low, value_low, preferred_element_type=jnp.float32
    )
    normed_grad = jnp.einsum("tk,dk->td", both_low, w_query_key, preferred_element_type=jnp.float32)
    normed_grad = normed_grad + jnp.einsum(
        "tk,dk->td", value_low, w_value, preferred_element_type=jnp.float32
    )
    through_one, gain_attn_grad = norm_backward(inputs, inverse_one, gain_attn, normed_grad)
    tokens_grad = (hidden_one_grad + through_one)[None]
    rel_bias_grad = bias_grad.T
    matrices = (w_query_key_grad, w_value_grad, w_attn_out_grad, w_in_grad, w_out_grad, w_proj_grad)
    partial_sums = (
        lax.psum_scatter(matrices[0], "rows", scatter_dimension=0, tiled=True),
        lax.psum_scatter(matrices[1], "rows", scatter_dimension=0, tiled=True),
        lax.psum_scatter(matrices[2], "rows", scatter_dimension=0, tiled=True),
        lax.psum_scatter(matrices[3], "rows", scatter_dimension=0, tiled=True),
        lax.psum_scatter(matrices[4], "rows", scatter_dimension=0, tiled=True),
        lax.psum_scatter(matrices[5], "rows", scatter_dimension=0, tiled=True),
    )
    summed = (
        lax.psum_scatter(
            partial_sums[0].astype(jnp.bfloat16), "tower", scatter_dimension=1, tiled=True
        ).astype(jnp.float32),
        lax.psum_scatter(
            partial_sums[1].astype(jnp.bfloat16), "tower", scatter_dimension=1, tiled=True
        ).astype(jnp.float32),
        lax.psum_scatter(
            partial_sums[2].astype(jnp.bfloat16), "tower", scatter_dimension=1, tiled=True
        ).astype(jnp.float32),
        lax.psum_scatter(
            partial_sums[3].astype(jnp.bfloat16), "tower", scatter_dimension=1, tiled=True
        ).astype(jnp.float32),
        lax.psum_scatter(
            partial_sums[4].astype(jnp.bfloat16), "tower", scatter_dimension=1, tiled=True
        ).astype(jnp.float32),
        lax.psum_scatter(
            partial_sums[5].astype(jnp.bfloat16), "tower", scatter_dimension=1, tiled=True
        ).astype(jnp.float32),
    )
    loss_sum = lax.psum(local_loss, ("tower", "rows"))
    small = lax.psum(
        (gain_attn_grad, gain_ff_grad, gain_final_grad, rel_bias_grad), ("tower", "rows")
    )
    loss = loss_sum / total_queries
    return (
        loss,
        tokens_grad,
        small[0],
        summed[0],
        summed[1],
        summed[2],
        small[3],
        small[1],
        summed[3],
        summed[4],
        small[2],
        summed[5],
    )


def solution(mesh):
    placed = (
        P("tower", "rows", None),
        P("rows", None),
        P("rows"),
        P(),
        P(),
        P(),
        P(),
        P(),
        P(),
        P(),
        P(),
        P(),
        P(),
        P(),
        P(),
    )
    return jax.shard_map(
        on_device,
        mesh=mesh,
        in_specs=placed,
        out_specs=(
            P(),
            P("tower", "rows", None),
            P(),
            P("rows", "tower"),
            P("rows", "tower"),
            P("rows", "tower"),
            P(),
            P(),
            P("rows", "tower"),
            P("rows", "tower"),
            P(),
            P("rows", "tower"),
        ),
        check_vma=False,
    )
```

profile of v0, /device:TPU:0, one launch (start us, length us, event | category | flops | bytes accessed | tf_op | source)
XLA Modules:
  0.0 1335.2 jit_solution(12893120904036431832)
XLA Ops:
  7.3 1.3 fusion.37
  8.6 1.9 convolution_convert_fusion.4
  10.6 0.9 copy.70
  12.2 215.6 %gather_fusion.1 = f32[65536,12]{1,0:T(8,128)} fusion(f32[12,511]{0,1:T(8,128)S(1)} %copy.74, s32[65536]{0:T(1024)S(1)} %broadcast_clamp_fusion.1), kind=kCustom, calls=%fused_computation.clone | custom fusion | bytes 6553600 | tf_op jit(solution)/shard_map/jit(_take)/gather | solution.py:28
  227.8 20.3 %copy.76 = f32[256,256,12]{0,1,2:T(8,128)} copy(f32[256,256,12]{2,1,0:T(8,128)} %bitcast.146) | data formatting | bytes 6291456 | tf_op jit(solution)/shard_map/jit(_take)/gather | solution.py:28
  248.9 0.8 convolution_convert_fusion
  250.7 1.3 copy.72
  253.0 2.8 fusion.93
  257.8 1.7 copy-done.12
  260.2 1.5 fusion.88
  261.9 2.0 multiply_reduce_fusion.5
  266.5 71.2 %all-gather = bf16[32,4,768]{2,1,0:T(4,128)(2,1)S(1)} all-gather(bf16[1,4,768]{2,1,0:T(4,128)(2,1)S(1)} %fusion.78), channel_id=1, replica_groups=mesh['tower'=2,'rows'=16] {'tower','rows'}, dimensions={0}, use_global_device_ids=true | all-gather | bytes 202752 | tf_op jit(solution)/shard_map/all_gather | solution.py:103
  339.7 1.4 copy.79
  341.1 1.3 eq.94
  342.4 1.6 reshape.305
  343.9 1.0 fusion.94
  346.2 1.3 subtract_multiply_fusion.1
  347.5 1.2 fusion.82
  348.7 1.2 multiply_reduce_fusion.7
  349.9 1.7 fusion.86
  351.6 2.9 multiply_reduce_fusion.1
  354.5 1.5 multiply_subtract_fusion
  356.1 5.4 fusion.10
  361.5 1.2 copy-done.21
  362.7 2.2 multiply_reduce_fusion.2
  365.2 0.9 copy-done.8
  366.3 1.2 convolution_convert_fusion.3
  367.5 1.9 copy.80
  369.4 2.6 fusion.19
  372.8 2.0 fusion.50
  374.8 3.1 fusion.66
  378.0 2.7 fusion.85
  380.8 3.1 multiply_reduce_fusion
  387.3 3.2 fusion.47
  390.8 8.0 fusion.69
  398.8 6.6 fusion.87
  406.5 690.1 %gather_fusion = s32[65536]{0:T(1024)} fusion(s32[511]{0:T(512)S(1)} %copy-done.1, s32[65536]{0:T(1024)S(1)} %broadcast_clamp_fusion), kind=kCustom, calls=%fused_computation.1 | custom fusion | bytes 786432 | tf_op jit(solution)/shard_map/jit(_take)/gather | solution.py:175
  1097.0 0.9 convert_element_type.165
  1098.8 1.0 and_select_fusion
  1099.9 3.7 copy.84
  1103.6 2.4 pad.5
  1106.0 4.5 copy.105
  1110.5 0.9 convert_element_type.167
  1112.3 6.0 fusion
  1118.3 0.9 convert_element_type.176
  1119.3 0.8 copy.97
  1120.8 1.6 convert_element_type.160
  1122.5 2.7 fusion.48
  1125.3 1.1 convert_element_type.174
  1126.4 0.9 copy.95
  1127.7 3.7 fusion.40
  1131.3 4.4 fusion.22
  1135.7 124.4 %reduce-scatter.29.cloned.1.call-done = f32[48,3072]{1,0:T(8,128)} async-done(((f32[768,3072]{1,0:T(8,128)}), f32[48,3072]{1,0:T(8,128)}) %reduce-scatter.29.cloned.1.call-update) | async-done | bytes 589840 | tf_op jit(solution)/shard_map/reduce_scatter | solution.py:217
  1260.1 1.8 convert_element_type.172
  1262.0 1.3 subtract_reduce_fusion
  1264.0 39.8 %all-reduce.1 = (f32[]{:T(128)}, f32[768]{0:T(1024)}, f32[32,12]{0,1:T(8,128)}, f32[768]{0:T(1024)}, f32[768]{0:T(1024)}) all-reduce(f32[]{:T(128)S(6)} %mul.352, f32[768]{0:T(1024)S(1)} %get-tuple-element.17, f32[32,12]{0,1:T(8,128)} %fusion.22, f32[768]{0:T(1024)} %get-tuple-element.15, ...), channel_id=1, replica_groups=mesh['tower'=2,'rows'=16] {'tower','rows'}, use_global_device_ids=true, to_apply=%region_11.13 | all-reduce | flops 2689 | bytes 21512 | tf_op jit(solution)/shard_map/psum | solution.py:241
  1305.2 2.3 fusion.36
  1307.5 1.0 copy.92
  1309.1 1.0 copy.94
  1310.7 1.0 copy.98
  1312.4 1.6 convert_element_type.161
  1313.9 1.1 copy.96
  1315.7 9.4 reduce-scatter.31.cloned.1.call-done
  1325.1 1.6 convert_element_type.173
  (202 shorter events, 23.9 us)
Async XLA Ops:
  7.2 241.7 %copy-start = (bf16[768,1536]{1,0:T(8,128)(2,1)S(1)}, bf16[768,1536]{1,0:T(8,128)(2,1)}, u32[]{:S(2)}) copy-start(bf16[768,1536]{1,0:T(8,128)(2,1)} %param.23) | copy-start | bytes 7077892
  7.2 4.3 copy-start.50
  7.2 4.3 copy-start.1
  7.2 1089.8 %reduce-scatter.25.cloned.1.call-start = ((), (), s32[]{:S(2)}) async-start(), calls=%async_computation.14 | async-start | bytes 2506752 | tf_op jit(solution)/shard_map/reduce_scatter | solution.py:215
  8.6 240.3 %copy-start.38 = (f32[256]{0:T(256)}, f32[256]{0:T(256)S(1)}, u32[]{:S(2)}) copy-start(f32[256]{0:T(256)S(1)} %add_rsqrt_fusion.2) | copy-start | bytes 3076
  227.8 21.1 %copy-start.5 = (bf16[1,256,768]{2,1,0:T(8,128)(2,1)S(1)}, bf16[1,256,768]{2,1,0:T(8,128)(2,1)}, u32[]{:S(2)}) copy-start(bf16[1,256,768]{2,1,0:T(8,128)(2,1)} %param.17) | copy-start | bytes 1179652
  227.8 21.1 %copy-start.32 = (f32[768]{0:T(1024)S(1)}, f32[768]{0:T(1024)}, u32[]{:S(2)}) copy-start(f32[768]{0:T(1024)} %param.22) | copy-start | bytes 9220
  248.9 3.8 copy-start.48
  250.7 5.1 copy-start.15
  252.1 3.8 copy-start.17
  252.8 11.3 copy-start.42
  255.8 2.0 copy-start.2
  255.9 1.3 copy-start.26
  255.9 4.3 slice-start
  257.1 2.4 copy-start.12
  257.1 3.1 slice-start.1
  257.1 3.1 copy-start.29
  257.8 2.3 copy-start.25
  259.6 2.3 slice-start.4
  260.2 1.5 copy-start.40
  260.2 1.7 slice-start.5
  261.9 2.0 copy-start.6
  261.9 2.9 copy-start.37
  261.9 3.5 copy-start.14
  264.0 0.9 copy-start.11
  264.0 75.1 %copy-start.43 = (f32[256]{0:T(256)}, f32[256]{0:T(256)S(1)}, u32[]{:S(2)}) copy-start(f32[256]{0:T(256)S(1)} %add_rsqrt_fusion) | copy-start | bytes 3076
  264.0 75.1 %copy-start.49 = (f32[4]{0:T(128)}, f32[4]{0:T(128)S(1)}, u32[]{:S(2)}) copy-start(f32[4]{0:T(128)S(1)} %broadcast_maximum_fusion) | copy-start | bytes 52
  265.4 73.7 %copy-start.36 = (bf16[4,768]{1,0:T(4,128)(2,1)}, bf16[4,768]{1,0:T(4,128)(2,1)S(1)}, u32[]{:S(2)}) copy-start(bf16[4,768]{1,0:T(4,128)(2,1)S(1)} %convolution_convert_fusion.5) | copy-start | bytes 18436
  265.9 73.2 %copy-start.30 = (f32[4,768]{1,0:T(4,128)}, f32[4,768]{1,0:T(4,128)S(1)}, u32[]{:S(2)}) copy-start(f32[4,768]{1,0:T(4,128)S(1)} %get-tuple-element.33) | copy-start | bytes 36868
  347.5 8.6 copy-start.7
  349.9 4.6 copy-start.35
  349.9 4.6 copy-start.45
  354.5 8.2 slice-start.2
  356.1 8.8 copy-start.10
  356.1 6.6 slice-start.3
  356.1 6.6 copy-start.41
  361.5 1.2 copy-start.21
  364.9 1.4 copy-start.13
  365.1 0.9 copy-start.8
  366.2 6.5 copy-start.39
  374.8 735.7 %reduce-scatter.27.cloned.1.call-start = ((), (), s32[]{:S(2)}) async-start(), calls=%async_computation.15 | async-start | bytes 2506752 | tf_op jit(solution)/shard_map/reduce_scatter | solution.py:216
  377.9 740.4 %reduce-scatter.35.cloned.1.call-start = ((), (), s32[]{:S(2)}) async-start(), calls=%async_computation.19 | async-start | bytes 2506752 | tf_op jit(solution)/shard_map/reduce_scatter | solution.py:219
  380.7 740.1 %reduce-scatter.21.cloned.1.call-start = ((), (), s32[]{:S(2)}) async-start(), calls=%async_computation.12 | async-start | bytes 5013504 | tf_op jit(solution)/shard_map/reduce_scatter | solution.py:214
  380.7 3.1 copy-start.3
  380.7 3.1 copy-start.31
  383.8 1.0 copy-start.16
  384.8 1.7 copy-start.4
  384.8 1.3 copy-start.18
  390.5 734.8 %reduce-scatter.33.cloned.1.call-start = ((), (), s32[]{:S(2)}) async-start(), calls=%async_computation.18 | async-start | bytes 10027008 | tf_op jit(solution)/shard_map/reduce_scatter | solution.py:218
  398.8 861.4 %reduce-scatter.29.cloned.1.call-start = ((), (), s32[]{:S(2)}) async-start(), calls=%async_computation.16 | async-start | bytes 10027008 | tf_op jit(solution)/shard_map/reduce_scatter | solution.py:217
  405.5 902.0 %reduce-scatter.37.cloned.1.call-start = ((), (), s32[]{:S(2)}) async-start(), calls=%async_computation.20 | async-start | bytes 294912
  1098.8 210.3 %reduce-scatter.39.cloned.1.call-start = ((), (), s32[]{:S(2)}) async-start(), calls=%async_computation.21 | async-start | bytes 294912
  1099.9 12.4 copy-start.27
  1110.5 9.7 copy-start.47
  1110.5 9.7 copy-start.34
  1111.4 11.1 copy-start.23
  1112.3 198.5 %reduce-scatter.43.cloned.1.call-start = ((), (), s32[]{:S(2)}) async-start(), calls=%async_computation.23 | async-start | bytes 294912
  1120.1 192.3 %reduce-scatter.23.cloned.1.call-start = ((), (), s32[]{:S(2)}) async-start(), calls=%async_computation.13 | async-start | bytes 221184 | tf_op jit(solution)/shard_map/reduce_scatter | solution.py:222
  1122.5 5.2 copy-start.20
  1122.5 191.5 %reduce-scatter.41.cloned.1.call-start = ((), (), s32[]{:S(2)}) async-start(), calls=%async_computation.22 | async-start | bytes 589824
  1127.3 197.8 %reduce-scatter.31.cloned.1.call-start = ((), (), s32[]{:S(2)}) async-start(), calls=%async_computation.17 | async-start | bytes 442368 | tf_op jit(solution)/shard_map/reduce_scatter | solution.py:231
  1127.7 3.7 copy-start.28
  1131.3 132.6 %copy-start.44 = (f32[768]{0:T(1024)S(1)}, f32[768]{0:T(1024)}, u32[]{:S(2)}) copy-start(f32[768]{0:T(1024)} %get-tuple-element.13) | copy-start | bytes 9220
  1131.3 173.8 %copy-start.9 = (f32[256,768]{1,0:T(8,128)S(1)}, f32[256,768]{1,0:T(8,128)}, u32[]{:S(2)}) copy-start(f32[256,768]{1,0:T(8,128)} %copy-done.8) | copy-start | bytes 2359300
  (5 other events, 3.4 us)
Sparse Core Ops, SparseCore 0:
  374.9 124.4 reduce-scatter.24
  505.1 127.5 reduce-scatter.26
  637.6 127.5 reduce-scatter.34
  771.0 136.9 reduce-scatter.20
  913.6 170.0 reduce-scatter.32
  1090.2 169.9 reduce-scatter.28
  1262.4 6.4 reduce-scatter.36
  1271.1 8.7 reduce-scatter.38
  1282.1 8.7 reduce-scatter.42
  1293.5 8.7 reduce-scatter.22
  1304.5 8.9 reduce-scatter.40
  1316.2 8.8 reduce-scatter.30
where the time goes:
time: 1340 us
  local copies, waits for them, and re-layouts  966 us (72%)
  waiting for transfers between devices  134 us (10%)
  blocking collectives  111 us (8%)
  matrix products  77.4 us (6%)
  other arithmetic  26.7 us (2%)
  between operations  18.6 us (1%)
    gather x1, local copies, waits for them, and re-layouts, on_device(): pair_bucket = jnp.take(bucket_table, offsets.reshape(-1))  690 us
    gather x2, local copies, waits for them, and re-layouts, block_scores(): biased = raw + jnp.take(table_rows, offsets, axis=1)  236 us
    reduce_scatter x1, waiting for transfers between devices, on_device(): lax.psum_scatter(matrices[3], 'rows', scatter_dimension=0, tiled=True)  124 us
    all_gather x1, blocking collectives, on_device(): gathered = lax.all_gather(embed_low, ('tower', 'rows'), axis=0, tiled=True)  71.2 us
    psum x1, blocking collectives, on_device(): loss_sum = lax.psum(local_loss, ('tower', 'rows'))  39.8 us
  transfers between devices with their start and end apart: 12, of which 2 were waited for; matrix products, arithmetic and copies ran while one was open for 58% of the time, Pallas kernels for 0%

commit v1 on v0

v1 whole, which is shorter than its diff:
```python
import math

import jax
import jax.numpy as jnp
from jax import lax
from jax.experimental import pallas as pl
from jax.experimental.pallas import tpu as pltpu
from jax.sharding import PartitionSpec as P

EPSILON = 1e-06
LOGIT_SCALE = 50.0
MASKED = -1000000000.0
MESH = pl.DeviceIdType.MESH
LOW = jnp.bfloat16
FULL = jnp.float32
LANES = 128
TILE = 512
UNIT_ROWS = 48
UNIT_COLUMNS = 384
VMEM_LIMIT = 60 * 2**20


def dot(left, right):
    return jnp.dot(left, right, preferred_element_type=FULL)


def dot_nt(left, right):
    return lax.dot_general(left, right, (((1,), (1,)), ((), ())), preferred_element_type=FULL)


def dot_tn(left, right):
    return lax.dot_general(left, right, (((0,), (0,)), ((), ())), preferred_element_type=FULL)


def split(values):
    upper = values.astype(LOW)
    return upper, (values - upper.astype(FULL)).astype(LOW)


def inverse_root(values):
    return lax.rsqrt(jnp.mean(values * values, axis=-1, keepdims=True) + EPSILON)


def norm_backward(values, inverse, gain, upstream):
    scaled = upstream * gain
    gain_grad = jnp.sum(upstream * (values * inverse), axis=0, keepdims=True)
    inner = jnp.mean(scaled * values, axis=-1, keepdims=True)
    return inverse * scaled - values * (inverse * inverse * inverse * inner), gain_grad


def tiles(total, size):
    def over(body):
        def step(index, carry):
            body(index, pl.ds(pl.multiple_of(index * size, size), size))
            return carry

        lax.fori_loop(0, total // size, step, 0)

    return over


class Refs:
    pass


def make_kernel(sizes, names):
    rows, width, model, ff, heads, buckets, per_row = sizes
    head_size = model // heads
    half = model // 2
    ff_half = ff // 2
    queries = rows * per_row
    parts = model // LANES
    query_message = parts * per_row
    row_bits = rows.bit_length() - 1

    def kernel(*args):
        r = Refs()
        for name, ref in zip(names, args):
            setattr(r, name, ref)
        tower = lax.axis_index("tower")
        row = lax.axis_index("rows")
        partner = (1 - tower, row)
        is_query = tower == 0

        barrier = pltpu.get_barrier_semaphore()
        pl.semaphore_signal(barrier, inc=1, device_id=partner, device_id_type=MESH)

        def greet(step, carry):
            peer = (tower, jnp.bitwise_xor(row, step))
            pl.semaphore_signal(barrier, inc=1, device_id=peer, device_id_type=MESH)
            return carry

        lax.fori_loop(1, rows, greet, 0)

        loads = {}
        for index, name in enumerate(("w_query_key", "w_value", "w_attn_out", "w_in", "w_out", "w_proj")):
            loads[name] = pltpu.make_async_copy(
                getattr(r, name), getattr(r, name + "_here"), r.load_sem.at[index]
            )
            loads[name].start()

        def weight(name):
            loads[name].wait()
            return getattr(r, name + "_here")

        def to_partner(src, dst, index):
            return pltpu.make_async_remote_copy(
                src_ref=src,
                dst_ref=dst,
                send_sem=r.core_send.at[index],
                recv_sem=r.core_recv.at[index],
                device_id=partner,
                device_id_type=MESH,
            )

        lane = lax.broadcasted_iota(jnp.int32, (8, width), 1)
        doc_row = jnp.where(lane < r.doc_lengths[0], 0, 1)
        seg_row = jnp.where(is_query, jnp.broadcast_to(r.query_segments[...], (8, width)), doc_row)
        eye = (
            lax.broadcasted_iota(jnp.int32, (width, width), 0)
            == lax.broadcasted_iota(jnp.int32, (width, width), 1)
        ).astype(FULL)
        seg_column = dot_nt(eye.astype(LOW), seg_row.astype(FULL).astype(LOW))[:, 0:1].astype(jnp.int32)
        member = (seg_row == lax.broadcasted_iota(jnp.int32, (8, width), 0)).astype(FULL)
        share = 1.0 / jnp.maximum(jnp.sum(member, axis=-1, keepdims=True), 1.0)

        wide = 2 * width
        table = jnp.concatenate(
            [r.bucket_table[...], jnp.zeros((1, 1), jnp.int32)], axis=1
        )
        turned = (
            lax.broadcasted_iota(jnp.int32, (wide, wide), 0)
            + lax.broadcasted_iota(jnp.int32, (wide, wide), 1)
            == wide - 2
        ).astype(FULL).astype(LOW)
        table_low = jnp.broadcast_to(table.astype(FULL), (8, wide)).astype(LOW)
        table_turned = dot(table_low, turned)[0:1]
        hot = (
            table_turned.astype(jnp.int32) == lax.broadcasted_iota(jnp.int32, (buckets, wide), 0)
        ).astype(FULL)
        r.hot[...] = hot.astype(LOW)
        bias_upper, bias_lower = split(r.rel_bias[...])
        bias_last = (r.rel_bias[...] - bias_upper.astype(FULL) - bias_lower.astype(FULL)).astype(LOW)
        hot_low = hot.astype(LOW)
        r.table[0:heads, :] = (
            dot_tn(bias_upper, hot_low) + dot_tn(bias_lower, hot_low) + dot_tn(bias_last, hot_low)
        )

        r.small[...] = jnp.zeros_like(r.small)
        r.diagonals[...] = jnp.zeros_like(r.diagonals)

        inputs = r.tokens[...].astype(FULL)
        normed = (inputs * inverse_root(inputs) * r.gain_attn[...]).astype(LOW)
        r.normed_one[0:width, :] = normed
        w_query_key = weight("w_query_key")

        @tiles(2 * model, TILE)
        def _(index, columns):
            r.qkv[:, columns] = dot(r.normed_one[0:width, :], w_query_key[:, columns]).astype(LOW)

        w_value = weight("w_value")
        r.qkv[:, 2 * model :] = dot(normed, w_value[...]).astype(LOW)

        pl.semaphore_wait(barrier, rows)
        send_one = to_partner(r.normed_one.at[0:width], r.normed_one.at[width : 2 * width], 0)
        send_one.start()

        r.keys_turned[...] = r.qkv[:, model : 2 * model].T
        r.values_turned[...] = r.qkv[:, 2 * model :].T

        allowed = seg_column == seg_row[0:1]
        r.allowed[...] = allowed.astype(FULL)

        @tiles(model, 2 * head_size)
        def _(pair, columns):
            query = r.qkv[:, columns]
            key = r.qkv[:, pl.ds(pl.multiple_of(model + pair * 2 * head_size, LANES), 2 * head_size)]
            place = lax.broadcasted_iota(jnp.int32, (width, 2 * head_size), 1)
            for side in range(2):
                head = 2 * pair + side
                own = (place >= head_size) if side else (place < head_size)
                score = dot_nt(jnp.where(own, key, jnp.zeros_like(key)), query)
                line = jnp.broadcast_to(r.table[pl.ds(head, 1), :], (width, wide))
                bias = pltpu.roll(line, width + 1, 1, stride=1, stride_axis=0)[:, :width]
                score = jnp.where(r.allowed[...] > 0.5, score + bias, MASKED)
                weights = jnp.exp(score - jnp.max(score, axis=0, keepdims=True))
                prob = (weights * (1.0 / jnp.sum(weights, axis=0, keepdims=True))).astype(LOW)
                r.probs[head] = prob
                here = pl.ds(pl.multiple_of(head * head_size, head_size), head_size)
                r.mixed_turned[here, :] = dot(r.values_turned[here, :], prob).astype(LOW)

        mixed = r.mixed_turned[...].T
        r.mixed[0:width, :] = mixed
        send_mixed = to_partner(r.mixed.at[0:width], r.mixed.at[width : 2 * width], 1)
        send_mixed.start()
        w_attn_out = weight("w_attn_out")
        hidden = r.tokens[...].astype(FULL) + dot(mixed, w_attn_out[...])
        r.hidden_one[...] = hidden
        r.normed_two[0:width, :] = (hidden * inverse_root(hidden) * r.gain_ff[...]).astype(LOW)
        send_two = to_partner(r.normed_two.at[0:width], r.normed_two.at[width : 2 * width], 2)
        send_two.start()

        w_in = weight("w_in")
        bend = math.sqrt(2.0 / math.pi)

        @tiles(ff, TILE)
        def _(index, columns):
            inner = dot(r.normed_two[0:width, :], w_in[:, columns])
            square = inner * inner
            curve = jnp.tanh(bend * (inner * (1.0 + 0.044715 * square)))
            lift = 0.5 * (1.0 + curve)
            r.active[0:width, columns] = (inner * lift).astype(LOW)
            slope = 0.5 * inner * (1.0 - curve * curve) * (bend * (1.0 + 3 * 0.044715 * square))
            r.slope[:, columns] = (lift + slope).astype(LOW)

        send_active = to_partner(r.active.at[0:width], r.active.at[width : 2 * width], 3)
        send_active.start()
        w_out = weight("w_out")

        @tiles(model, model // 3)
        def _(index, columns):
            r.hidden_two[:, columns] = r.hidden_one[:, columns] + dot(
                r.active[0:width, :], w_out[:, columns]
            )

        hidden = r.hidden_two[...]
        normed_upper, normed_lower = split(hidden * inverse_root(hidden) * r.gain_final[...])
        member_low = member.astype(LOW)
        pooled = (dot(member_low, normed_upper) + dot(member_low, normed_lower)) * share
        pooled = pooled.astype(LOW).astype(FULL)

        own_queries = r.pooled_queries.at[pl.ds(pl.multiple_of(row * query_message, 8), query_message)]
        own_doc = r.pooled_docs.at[pl.ds(pl.multiple_of(row * 8, 8), 8)]

        def spread(block, act):
            def step(index, carry):
                act(
                    pltpu.make_async_remote_copy(
                        src_ref=block,
                        dst_ref=block,
                        send_sem=r.spread_send.at[index],
                        recv_sem=r.spread_recv.at[index],
                        device_id=(tower, jnp.bitwise_xor(row, index)),
                        device_id_type=MESH,
                    )
                )
                return carry

            lax.fori_loop(1, rows, step, 0)

        relay_queries = to_partner(r.pooled_queries, r.pooled_queries, 4)
        relay_docs = to_partner(r.pooled_docs, r.pooled_docs, 5)

        @pl.when(is_query)
        def _():
            for part in range(parts):
                spot = pl.multiple_of(row * query_message, 8) + part * per_row
                r.pooled_queries[pl.ds(spot, per_row), :] = pooled[
                    0:per_row, part * LANES : (part + 1) * LANES
                ]
            spread(own_queries, lambda copy: copy.start())
            spread(own_queries, lambda copy: copy.wait())
            relay_queries.start()
            relay_docs.wait_recv()
            relay_queries.wait_send()

        @pl.when(jnp.logical_not(is_query))
        def _():
            own_doc[...] = jnp.zeros((8, LANES), FULL)
            for part in range(parts):
                spot = pl.multiple_of(row * 8, 8) + part
                r.pooled_docs[pl.ds(spot, 1), :] = pooled[0:1, part * LANES : (part + 1) * LANES]
            spread(own_doc, lambda copy: copy.start())
            spread(own_doc, lambda copy: copy.wait())
            relay_docs.start()
            relay_queries.wait_recv()
            relay_docs.wait_send()

        for part in range(parts):
            lanes = slice(part * LANES, (part + 1) * LANES)
            for query in range(per_row):
                r.pooled[query * rows : (query + 1) * rows, lanes] = r.pooled_queries[
                    pl.ds(part * per_row + query, rows, stride=query_message), :
                ]
            r.pooled[queries:, lanes] = r.pooled_docs[pl.ds(part, rows, stride=8), :]

        w_proj = weight("w_proj")
        pooled_low = r.pooled[...].astype(LOW)
        projected = dot(pooled_low, w_proj[...])
        scale = lax.rsqrt(jnp.sum(projected * projected, axis=-1, keepdims=True) + EPSILON)
        embed = (projected * scale).astype(LOW)
        query_embed, doc_embed = embed[:queries], embed[queries:]
        logits = LOGIT_SCALE * dot_nt(query_embed, doc_embed)
        target = jnp.concatenate(
            [
                (
                    r.positives[:, query : query + 1]
                    == lax.broadcasted_iota(jnp.int32, (rows, rows), 1)
                ).astype(FULL)
                for query in range(per_row)
            ],
            axis=0,
        )
        highest = jnp.max(logits, axis=-1, keepdims=True)
        log_sum = highest + jnp.log(jnp.sum(jnp.exp(logits - highest), axis=-1, keepdims=True))
        missed = log_sum - jnp.sum(logits * target, axis=-1, keepdims=True)
        r.loss[...] = jnp.sum(missed, axis=0, keepdims=True) / queries
        logits_grad = (jnp.exp(logits - log_sum) - target) * (LOGIT_SCALE / queries)
        grad_upper, grad_lower = split(logits_grad)
        embed_grad = jnp.concatenate(
            [
                dot(grad_upper, doc_embed) + dot(grad_lower, doc_embed),
                dot_tn(grad_upper, query_embed) + dot_tn(grad_lower, query_embed),
            ],
            axis=0,
        )
        along = jnp.sum(embed_grad * projected, axis=-1, keepdims=True)
        proj_grad = (scale * embed_grad - projected * (scale * scale * scale * along)).astype(LOW)
        r.proj_grad[...] = proj_grad.astype(FULL)
        r.own_grad[...] = jnp.zeros_like(r.own_grad)

        @pl.when(is_query)
        def _():
            for query in range(per_row):
                r.own_grad[query : query + 1, :] = r.proj_grad[pl.ds(query * rows + row, 1), :]

        @pl.when(jnp.logical_not(is_query))
        def _():
            r.own_grad[0:1, :] = r.proj_grad[pl.ds(queries + row, 1), :]

        pooled_grad = dot_nt(r.own_grad[...].astype(LOW), w_proj[...])[0:8] * share
        final_grad = jnp.zeros((width, model), FULL)
        for query in range(per_row):
            final_grad = jnp.where(seg_column == query, pooled_grad[query : query + 1, :], final_grad)

        hidden = r.hidden_two[...]
        hidden_grad, r.small[2:3, :] = norm_backward(
            hidden, inverse_root(hidden), r.gain_final[...], final_grad
        )
        r.hidden_grad[...] = hidden_grad
        r.branch[...] = hidden_grad.astype(LOW)
        own_half = pl.ds(pl.multiple_of(tower * half, LANES), half)
        other_half = pl.ds(pl.multiple_of((1 - tower) * half, LANES), half)
        send_branch = to_partner(r.branch.at[:, other_half], r.branch_half.at[width : 2 * width], 6)
        send_branch.start()
        r.branch_half[0:width, :] = r.branch[:, own_half]

        r.proj_grad_half[...] = r.proj_grad[:, own_half].astype(LOW)
        r.w_proj_whole[...] = dot_tn(r.pooled[...].astype(LOW), r.proj_grad_half[...])

        @tiles(ff, TILE)
        def _(index, columns):
            active_grad = dot_nt(r.branch[...], w_out[columns, :])
            r.inner_grad[:, columns] = (active_grad * r.slope[:, columns].astype(FULL)).astype(LOW)

        own_ff = pl.ds(pl.multiple_of(tower * ff_half, LANES), ff_half)
        other_ff = pl.ds(pl.multiple_of((1 - tower) * ff_half, LANES), ff_half)
        send_inner = to_partner(r.inner_grad.at[:, other_ff], r.inner_half.at[width : 2 * width], 7)
        send_inner.start()
        r.inner_half[0:width, :] = r.inner_grad[:, own_ff]

        send_active.wait()
        send_branch.wait()

        @tiles(ff, model)
        def _(index, columns):
            r.out_parts[index] = dot_tn(r.active[:, columns], r.branch_half[...]).astype(LOW)

        @tiles(model, model // 3)
        def _(index, columns):
            r.normed_grad[:, columns] = dot_nt(r.inner_grad[...], w_in[columns, :])

        hidden = r.hidden_one[...]
        through, r.small[1:2, :] = norm_backward(
            hidden, inverse_root(hidden), r.gain_ff[...], r.normed_grad[...]
        )
        hidden_grad = r.hidden_grad[...] + through
        r.hidden_grad[...] = hidden_grad
        r.attn[...] = hidden_grad.astype(LOW)
        send_attn = to_partner(r.attn.at[:, other_half], r.attn_half.at[width : 2 * width], 8)
        send_attn.start()
        r.attn_half[0:width, :] = r.attn[:, own_half]

        send_two.wait()
        send_inner.wait()

        @tiles(ff_half, TILE)
        def _(index, columns):
            r.in_parts[index] = dot_tn(r.normed_two[...], r.inner_half[:, columns]).astype(LOW)

        r.mixed_grad[...] = dot_nt(r.attn[...], w_attn_out[...]).astype(LOW)
        send_mixed.wait()
        send_attn.wait()
        r.attn_parts[...] = dot_tn(r.mixed[...], r.attn_half[...]).astype(LOW)

        @tiles(model, 2 * head_size)
        def _(pair, columns):
            query = r.qkv[:, columns]
            value = r.qkv[:, pl.ds(pl.multiple_of(2 * model + pair * 2 * head_size, LANES), 2 * head_size)]
            mixed_grad = r.mixed_grad[:, columns]
            place = lax.broadcasted_iota(jnp.int32, (width, 2 * head_size), 1)
            key_sides, value_sides = [], []
            for side in range(2):
                head = 2 * pair + side
                own = (place >= head_size) if side else (place < head_size)
                prob_low = r.probs[head]
                prob = prob_low.astype(FULL)
                prob_grad = dot_nt(jnp.where(own, value, jnp.zeros_like(value)), mixed_grad)
                weighted = prob * prob_grad
                score_grad = weighted - prob * jnp.sum(weighted, axis=0, keepdims=True)
                score_low = score_grad.astype(LOW)
                key_sides.append(dot(score_low, query))
                value_sides.append(dot(prob_low, mixed_grad))
                here = pl.ds(pl.multiple_of(head * head_size, head_size), head_size)
                r.queries_turned[here, :] = dot(r.keys_turned[here, :], score_low).astype(LOW)
                r.score_grad[...] = score_grad
                total = jnp.zeros((8, wide), FULL)
                blank = jnp.zeros((8, wide - width), FULL)
                for block in range(width // 8):
                    line = jnp.concatenate([r.score_grad[8 * block : 8 * block + 8, :], blank], axis=1)
                    total = total + pltpu.roll(line, (wide + width - 1 - 8 * block) % wide, 1)
                for line in range(8):
                    r.diagonals[line, pl.ds(head, 1), :] = total[line : line + 1, :]
            after = place >= head_size
            r.qkv_grad[:, pl.ds(pl.multiple_of(model + pair * 2 * head_size, LANES), 2 * head_size)] = (
                jnp.where(after, key_sides[1], key_sides[0]).astype(LOW)
            )
            r.qkv_grad[:, pl.ds(pl.multiple_of(2 * model + pair * 2 * head_size, LANES), 2 * head_size)] = (
                jnp.where(after, value_sides[1], value_sides[0]).astype(LOW)
            )

        r.qkv_grad[:, 0:model] = r.queries_turned[...].T

        own_whole = pl.ds(pl.multiple_of(tower * model, LANES), model)
        other_whole = pl.ds(pl.multiple_of((1 - tower) * model, LANES), model)
        own_value = pl.ds(pl.multiple_of(2 * model + tower * half, LANES), half)
        other_value = pl.ds(pl.multiple_of(2 * model + (1 - tower) * half, LANES), half)
        send_qk = to_partner(
            r.qkv_grad.at[:, other_whole], r.qkv_half.at[width : 2 * width, 0:model], 9
        )
        send_value = to_partner(
            r.qkv_grad.at[:, other_value], r.qkv_half.at[width : 2 * width, model:], 10
        )
        send_qk.start()
        send_value.start()
        r.qkv_half[0:width, 0:model] = r.qkv_grad[:, own_whole]
        r.qkv_half[0:width, model:] = r.qkv_grad[:, own_value]

        normed_grad = dot_nt(r.qkv_grad[:, 0 : 2 * model], w_query_key[...])
        r.normed_grad[...] = normed_grad + dot_nt(r.qkv_grad[:, 2 * model :], w_value[...])
        inputs = r.tokens[...].astype(FULL)
        through, r.small[0:1, :] = norm_backward(
            inputs, inverse_root(inputs), r.gain_attn[...], r.normed_grad[...]
        )
        r.tokens_grad[...] = r.hidden_grad[...] + through

        offsets = jnp.zeros((16, wide), FULL)
        for line in range(8):
            row_lines = r.diagonals[line]
            offsets = offsets + (pltpu.roll(row_lines, wide - line, 1) if line else row_lines)
        offset_upper, offset_lower = split(offsets)
        hot_low = r.hot[...]
        r.small[8 : 8 + buckets, 0:16] = dot_nt(hot_low, offset_upper) + dot_nt(hot_low, offset_lower)

        send_one.wait()
        send_qk.wait()
        send_value.wait()
        r.qkv_parts[...] = dot_tn(r.normed_one[...], r.qkv_half[...]).astype(LOW)

        small_rows = 8 + buckets
        for bit in range(row_bits + 1):
            peer = partner if bit == row_bits else (tower, jnp.bitwise_xor(row, 1 << bit))
            copy = pltpu.make_async_remote_copy(
                src_ref=r.small,
                dst_ref=r.small_in.at[bit],
                send_sem=r.small_send.at[bit],
                recv_sem=r.small_recv.at[bit],
                device_id=peer,
                device_id_type=MESH,
            )
            copy.start()
            copy.wait()
            r.small[...] = r.small[...] + r.small_in[bit]
        r.gain_attn_grad[...] = r.small[0:1, :]
        r.gain_ff_grad[...] = r.small[1:2, :]
        r.gain_final_grad[...] = r.small[2:3, :]
        r.rel_bias_grad[...] = r.small[8 : 8 + buckets, 0:heads]

    return kernel


def on_device(rows):
    def step(
        tokens,
        query_segments,
        doc_lengths,
        bucket_table,
        positives,
        gain_attn,
        w_query_key,
        w_value,
        w_attn_out,
        rel_bias,
        gain_ff,
        w_in,
        w_out,
        gain_final,
        w_proj,
    ):
        width, model = tokens.shape[1:]
        ff = w_in.shape[1]
        buckets, heads = rel_bias.shape
        per_row = positives.shape[1]
        half = model // 2
        wide = 2 * width
        queries = rows * per_row
        row_bits = rows.bit_length() - 1
        own_rows = model // rows
        vmem = pl.BlockSpec(memory_space=pltpu.VMEM)
        smem = pl.BlockSpec(memory_space=pltpu.SMEM)
        hbm = pl.BlockSpec(memory_space=pl.ANY)
        inputs = [
            ("tokens", tokens[0], vmem),
            ("query_segments", query_segments, vmem),
            ("doc_lengths", doc_lengths, smem),
            ("bucket_table", bucket_table[None], vmem),
            ("positives", positives, vmem),
            ("gain_attn", gain_attn[None], vmem),
            ("w_query_key", w_query_key, hbm),
            ("w_value", w_value, hbm),
            ("w_attn_out", w_attn_out, hbm),
            ("rel_bias", rel_bias, vmem),
            ("gain_ff", gain_ff[None], vmem),
            ("w_in", w_in, hbm),
            ("w_out", w_out, hbm),
            ("gain_final", gain_final[None], vmem),
            ("w_proj", w_proj, hbm),
        ]
        outputs = [
            ("loss", (1, 1), FULL),
            ("tokens_grad", (width, model), FULL),
            ("gain_attn_grad", (1, model), FULL),
            ("gain_ff_grad", (1, model), FULL),
            ("gain_final_grad", (1, model), FULL),
            ("rel_bias_grad", (buckets, heads), FULL),
            ("w_proj_whole", (model, half), FULL),
            ("out_parts", (ff // model, model, half), LOW),
            ("in_parts", (ff // 2 // TILE, model, TILE), LOW),
            ("attn_parts", (model, half), LOW),
            ("qkv_parts", (model, model + half), LOW),
        ]
        scratch = [
            ("w_query_key_here", w_query_key.shape, LOW),
            ("w_value_here", w_value.shape, LOW),
            ("w_attn_out_here", w_attn_out.shape, LOW),
            ("w_in_here", w_in.shape, LOW),
            ("w_out_here", w_out.shape, LOW),
            ("w_proj_here", w_proj.shape, LOW),
            ("hot", (buckets, wide), LOW),
            ("table", (16, wide), FULL),
            ("allowed", (width, width), FULL),
            ("normed_one", (2 * width, model), LOW),
            ("qkv", (width, 3 * model), LOW),
            ("keys_turned", (model, width), LOW),
            ("values_turned", (model, width), LOW),
            ("probs", (heads, width, width), LOW),
            ("mixed_turned", (model, width), LOW),
            ("mixed", (2 * width, model), LOW),
            ("hidden_one", (width, model), FULL),
            ("normed_two", (2 * width, model), LOW),
            ("active", (2 * width, ff), LOW),
            ("slope", (width, ff), LOW),
            ("hidden_two", (width, model), FULL),
            ("pooled_queries", (rows * per_row * model // LANES, LANES), FULL),
            ("pooled_docs", (rows * 8, LANES), FULL),
            ("pooled", (queries + rows, model), FULL),
            ("proj_grad", (queries + rows, model), FULL),
            ("proj_grad_half", (queries + rows, half), LOW),
            ("own_grad", (16, model), FULL),
            ("hidden_grad", (width, model), FULL),
            ("branch", (width, model), LOW),
            ("branch_half", (2 * width, half), LOW),
            ("inner_grad", (width, ff), LOW),
            ("inner_half", (2 * width, ff // 2), LOW),
            ("normed_grad", (width, model), FULL),
            ("attn", (width, model), LOW),
            ("attn_half", (2 * width, half), LOW),
            ("mixed_grad", (width, model), LOW),
            ("score_grad", (width, width), FULL),
            ("diagonals", (8, 16, wide), FULL),
            ("queries_turned", (model, width), LOW),
            ("qkv_grad", (width, 3 * model), LOW),
            ("qkv_half", (2 * width, model + half), LOW),
            ("small", (8 + buckets, model), FULL),
            ("small_in", (row_bits + 1, 8 + buckets, model), FULL),
        ]
        semaphores = [
            ("load_sem", 6),
            ("core_send", 11),
            ("core_recv", 11),
            ("spread_send", rows),
            ("spread_recv", rows),
            ("small_send", row_bits + 1),
            ("small_recv", row_bits + 1),
        ]
        names = [name for group in (inputs, outputs, scratch, semaphores) for name, *_ in group]
        sizes = (rows, width, model, ff, heads, buckets, per_row)
        results = pl.pallas_call(
            make_kernel(sizes, names),
            out_shape=[jax.ShapeDtypeStruct(shape, kind) for _, shape, kind in outputs],
            in_specs=[spec for _, _, spec in inputs],
            out_specs=[vmem] * len(outputs),
            scratch_shapes=[pltpu.VMEM(shape, kind) for _, shape, kind in scratch]
            + [pltpu.SemaphoreType.DMA((count,)) for _, count in semaphores],
            compiler_params=pltpu.CompilerParams(
                collective_id=0, has_side_effects=True, vmem_limit_bytes=VMEM_LIMIT
            ),
        )(*[array for _, array, _ in inputs])
        r = dict(zip([name for name, *_ in outputs], results))

        def over_rows(parts, axis):
            return lax.psum_scatter(parts, "rows", scatter_dimension=axis, tiled=True).astype(FULL)

        out_grad = over_rows(r["out_parts"].reshape(ff, half), 0)
        in_grad = over_rows(r["in_parts"], 1).transpose(1, 0, 2).reshape(own_rows, ff // 2)
        attn_grad = over_rows(r["attn_parts"], 0)
        qkv_grad = over_rows(r["qkv_parts"], 0)
        return (
            r["loss"][0, 0],
            r["tokens_grad"][None],
            r["gain_attn_grad"][0],
            qkv_grad[:, :model],
            qkv_grad[:, model:],
            attn_grad,
            r["rel_bias_grad"],
            r["gain_ff_grad"][0],
            in_grad,
            out_grad,
            r["gain_final_grad"][0],
            lax.dynamic_slice_in_dim(
                r["w_proj_whole"], lax.axis_index("rows") * own_rows, own_rows, 0
            ),
        )

    return step


def solution(mesh):
    return jax.shard_map(
        on_device(mesh.shape["rows"]),
        mesh=mesh,
        in_specs=(P("tower", "rows", None), P("rows", None), P("rows")) + (P(),) * 12,
        out_specs=(
            P(),
            P("tower", "rows", None),
            P(),
            P("rows", "tower"),
            P("rows", "tower"),
            P("rows", "tower"),
            P(),
            P(),
            P("rows", "tower"),
            P("rows", "tower"),
            P(),
            P("rows", "tower"),
        ),
        check_vma=False,
    )
```

time: 1340 us -> 613 us (0.46)
  local copies, waits for them, and re-layouts: 966 us -> 13.4 us
  waiting for transfers between devices: 134 us -> 506 us
  blocking collectives: 111 us -> 0 us
  matrix products: 77.4 us -> 0 us
  Pallas kernels: 0 us -> 70.4 us
  other arithmetic: 26.7 us -> 5.79 us
    gather x3 -> x0, local copies, waits for them, and re-layouts: 926 us -> none  [the longest x1 690 us: on_device(): pair_bucket = jnp.take(bucket_table, offsets.reshape(-1))]
    reduce_scatter x8 -> x4, waiting for transfers between devices: 134 us -> 504 us  [over_rows(): lax.psum_scatter(parts, 'rows', scatter_dimension=axis, tiled=True)]
    dot_general x32 -> x0, matrix products: 77.4 us -> none  [the longest x1 8 us: on_device(): jnp.einsum('tf,td->fd', active_low, branch_low, preferred_element_type=jn...]
    all_gather x1 -> x0, blocking collectives: 71.2 us -> none  [on_device(): gathered = lax.all_gather(embed_low, ('tower', 'rows'), axis=0, tiled=True)]
    pallas_call x0 -> x1, Pallas kernels: none -> 70.4 us  [step(): pl.pallas_call(make_kernel(sizes, names), out_shape=[jax.ShapeDtypeStruct...]
    psum x1 -> x0, blocking collectives: 39.8 us -> none  [on_device(): loss_sum = lax.psum(local_loss, ('tower', 'rows'))]
    unnamed x130 -> x14, local copies, waits for them, and re-layouts: 26.4 us -> 4.41 us
  transfers between devices with their start and end apart: 12 -> 4, of which waited for: 2 -> 4; matrix products, arithmetic and copies ran while one was open for 58% -> 2% of each run, Pallas kernels for 0% -> 0%
where the time goes in v1:
time: 613 us; the launch traced here: 612 us
  waiting for transfers between devices  506 us (83%)
  Pallas kernels  70.4 us (11%)
  between operations  16.3 us (3%)
  local copies, waits for them, and re-layouts  13.4 us (2%)
    reduce_scatter x4, waiting for transfers between devices, over_rows(): lax.psum_scatter(parts, 'rows', scatter_dimension=axis, tiled=True)  504 us
    pallas_call x1, Pallas kernels, step(): pl.pallas_call(make_kernel(sizes, names), out_shape=[jax.ShapeDtypeStruct...  70.4 us
  transfers between devices with their start and end apart: 4, of which 4 were waited for; matrix products, arithmetic and copies ran while one was open for 2% of the time, Pallas kernels for 0%

profile of v1, /device:TPU:0, one launch (start us, length us, event | category | flops | bytes accessed | tf_op | source)
XLA Modules:
  0.0 612.1 jit_solution(13639283480110923440)
XLA Ops:
  7.2 0.0 reduce-scatter.7.cloned.1.call-start
  7.2 1.4 copy.31.args_9_
  8.6 1.4 copy.30.args_4_
  10.0 1.3 broadcast_in_dim.16.args_5_
  11.2 1.3 broadcast_in_dim.17.args_10_
  12.5 1.3 broadcast_in_dim.18.args_13_
  14.4 70.4 %shard_map.238 = (f32[1,1]{1,0:T(1,128)}, f32[256,768]{1,0:T(8,128)}, f32[1,768]{1,0:T(1,128)}, f32[1,768]{1,0:T(1,128)}, f32[1,768]{1,0:T(1,128)}, /*index=5*/f...) custom-call(bf16[256,768]{1,0:T(8,128)(2,1)} %bitcast.11, ...), custom_call_target="tpu_custom_call" | custom-call | tf_op jit(solution)/shard_map/pallas_call | solution.py:608
  84.9 0.0 reduce-scatter.7.cloned.1.call-update
  84.9 0.0 reduce-scatter.5.cloned.1.call-start
  84.9 0.7 reduce-scatter.5.cloned.1.call-update
  85.6 0.0 reduce-scatter.9.cloned.1.call-start
  85.7 0.7 reduce-scatter.9.cloned.1.call-update
  86.4 0.0 copy-start.1
  86.4 0.0 copy-start.4
  86.4 0.0 copy-start.3
  86.4 0.0 copy-start.2
  86.4 0.0 reduce-scatter.11.cloned.1.call-start
  86.5 0.0 copy-start
  86.5 0.5 reduce-scatter.11.cloned.1.call-update
  87.0 0.1 copy-done.1
  87.1 0.7 copy.33
  87.8 0.0 copy-done.4
  87.8 0.6 reduce
  88.4 0.0 copy-done.3
  88.4 0.6 reduce.1
  89.0 0.0 copy-done.2
  89.0 0.6 reduce.2
  89.6 1.5 constant_dynamic-slice_fusion
  91.1 115.3 %reduce-scatter.7.cloned.1.call-done = bf16[48,384]{1,0:T(8,128)(2,1)} async-done(((bf16[768,384]{1,0:T(8,128)(2,1)}), bf16[48,384]{1,0:T(8,128)(2,1)}) %reduce-scatter.7.cloned.1.call-update) | async-done | bytes 36880 | tf_op jit(solution)/shard_map/reduce_scatter | solution.py:622
  206.4 1.4 convert_element_type.11
  207.8 129.7 %reduce-scatter.5.cloned.1.call-done = bf16[48,1152]{1,0:T(8,128)(2,1)} async-done(((bf16[768,1152]{1,0:T(8,128)(2,1)}), bf16[48,1152]{1,0:T(8,128)(2,1)}) %reduce-scatter.5.cloned.1.call-update) | async-done | bytes 110608 | tf_op jit(solution)/shard_map/reduce_scatter | solution.py:622
  337.5 1.6 slice.8
  339.1 1.4 slice.9
  340.5 129.3 %reduce-scatter.9.cloned.1.call-done = bf16[3,48,512]{2,1,0:T(8,128)(2,1)} async-done(((bf16[3,768,512]{2,1,0:T(8,128)(2,1)}), bf16[3,48,512]{2,1,0:T(8,128)(2,1)}) %reduce-scatter.9.cloned.1.call-update) | async-done | bytes 147472 | tf_op jit(solution)/shard_map/reduce_scatter | solution.py:622
  469.7 0.9 convert_bitcast_fusion
  470.7 0.7 copy.34
  471.4 129.8 %reduce-scatter.11.cloned.1.call-done = bf16[192,384]{1,0:T(8,128)(2,1)} async-done(((bf16[3072,384]{1,0:T(8,128)(2,1)}), bf16[192,384]{1,0:T(8,128)(2,1)}) %reduce-scatter.11.cloned.1.call-update) | async-done | bytes 147472 | tf_op jit(solution)/shard_map/reduce_scatter | solution.py:622
  601.2 1.6 convert_element_type.12
  603.5 0.0 copy-done
  603.5 0.9 copy.39
Async XLA Ops:
  7.2 199.2 %reduce-scatter.7.cloned.1.call-start = ((), (), s32[]{:S(2)}) async-start(), calls=%async_computation.5 | async-start | bytes 626688 | tf_op jit(solution)/shard_map/reduce_scatter | solution.py:622
  84.9 252.6 %reduce-scatter.5.cloned.1.call-start = ((), (), s32[]{:S(2)}) async-start(), calls=%async_computation.4 | async-start | bytes 1880064 | tf_op jit(solution)/shard_map/reduce_scatter | solution.py:622
  85.6 384.1 %reduce-scatter.9.cloned.1.call-start = ((), (), s32[]{:S(2)}) async-start(), calls=%async_computation.6 | async-start | bytes 2506752 | tf_op jit(solution)/shard_map/reduce_scatter | solution.py:622
  86.4 0.7 copy-start.1
  86.4 1.4 copy-start.4
  86.4 2.0 copy-start.3
  86.4 2.6 copy-start.2
  86.4 514.8 %reduce-scatter.11.cloned.1.call-start = ((), (), s32[]{:S(2)}) async-start(), calls=%async_computation.7 | async-start | bytes 2506752 | tf_op jit(solution)/shard_map/reduce_scatter | solution.py:622
  86.5 517.1 %copy-start = (f32[256,768]{1,0:T(8,128)S(1)}, f32[256,768]{1,0:T(8,128)}, u32[]{:S(2)}) copy-start(f32[256,768]{1,0:T(8,128)} %get-tuple-element.24) | copy-start | bytes 2359300
Sparse Core Ops, SparseCore 0:
  85.0 121.3 reduce-scatter.6
  212.0 125.4 reduce-scatter.4
  343.2 126.4 reduce-scatter.8
  474.5 126.6 reduce-scatter.10

commit v2 on v1

--- a/solution.py
+++ b/solution.py
@@ -1,4 +1,5 @@
 import math
+from types import SimpleNamespace
 
 import jax
 import jax.numpy as jnp
@@ -15,9 +16,19 @@
 FULL = jnp.float32
 LANES = 128
 TILE = 512
-UNIT_ROWS = 48
-UNIT_COLUMNS = 384
 VMEM_LIMIT = 60 * 2**20
+
+Z_HALF, Z_PAIR, Y, X = range(4)
+X_FIRST = (X, Y, Z_PAIR, Z_HALF)
+Y_FIRST = (Y, X, Z_PAIR, Z_HALF)
+Z_THEN_X = (Z_PAIR, X, Y, Z_HALF)
+Z_THEN_Y = (Z_PAIR, Y, X, Z_HALF)
+ORDERS = (
+    X_FIRST, Y_FIRST, Z_THEN_X, X_FIRST, Y_FIRST, Z_THEN_Y,
+    X_FIRST, Y_FIRST, Z_THEN_X, X_FIRST, Y_FIRST, Z_THEN_Y,
+)
+AFTER_STAGE = (0, 0, 3, 3, 3, 3)
+OUT_UNIT, IN_UNIT, ATTN_UNIT, QKV_UNIT, UNITS = 0, 4, 8, 9, 12
 
 
 def dot(left, right):
@@ -59,8 +70,8 @@
     return over
 
 
-class Refs:
-    pass
+def in_kernel_sums(rows, model):
+    return rows == 2 ** len(ORDERS[0]) and model % (16 * rows) == 0
 
 
 def make_kernel(sizes, names):
@@ -72,15 +83,16 @@
     parts = model // LANES
     query_message = parts * per_row
     row_bits = rows.bit_length() - 1
+    direct = in_kernel_sums(rows, model)
 
     def kernel(*args):
-        r = Refs()
-        for name, ref in zip(names, args):
-            setattr(r, name, ref)
+        r = SimpleNamespace(**dict(zip(names, args)))
+        arrived = args[len(names) :]
         tower = lax.axis_index("tower")
         row = lax.axis_index("rows")
         partner = (1 - tower, row)
         is_query = tower == 0
+        own_rows = model // rows
 
         barrier = pltpu.get_barrier_semaphore()
         pl.semaphore_signal(barrier, inc=1, device_id=partner, device_id_type=MESH)
@@ -92,16 +104,21 @@
 
         lax.fori_loop(1, rows, greet, 0)
 
-        loads = {}
-        for index, name in enumerate(("w_query_key", "w_value", "w_attn_out", "w_in", "w_out", "w_proj")):
-            loads[name] = pltpu.make_async_copy(
-                getattr(r, name), getattr(r, name + "_here"), r.load_sem.at[index]
-            )
-            loads[name].start()
-
-        def weight(name):
-            loads[name].wait()
-            return getattr(r, name + "_here")
+        loads = [
+            pltpu.make_async_copy(far, near, r.load_sem.at[index])
+            for index, (far, near) in enumerate(
+                (
+                    (r.w_query_key, r.w_query_key_here),
+                    (r.w_value, r.w_value_here),
+                    (r.w_attn_out, r.w_attn_out_here),
+                    (r.w_in, r.w_in_here),
+                    (r.w_out, r.w_out_here),
+                    (r.w_proj, r.w_proj_here),
+                )
+            )
+        ]
+        for load in loads:
+            load.start()
 
         def to_partner(src, dst, index):
             return pltpu.make_async_remote_copy(
@@ -112,6 +129,69 @@
                 device_id=partner,
                 device_id_type=MESH,
             )
+
+        coordinate = [jnp.bitwise_and(lax.shift_right_logical(row, 3 - bit), 1) for bit in range(4)]
+
+        def piece(unit, phase, kept):
+            order = ORDERS[unit]
+            place = [slice(None)] * 4
+            for bit in order[:phase]:
+                place[bit] = coordinate[bit]
+            last = order[phase]
+            place[last] = coordinate[last] if kept else 1 - coordinate[last]
+            return (unit, *place)
+
+        def exchange(unit, phase):
+            return pltpu.make_async_remote_copy(
+                src_ref=r.grads.at[piece(unit, phase, False)],
+                dst_ref=arrived[phase].at[unit],
+                send_sem=r.sum_send.at[unit, phase],
+                recv_sem=r.sum_recv.at[unit, phase],
+                device_id=(tower, jnp.bitwise_xor(row, 1 << (3 - ORDERS[unit][phase]))),
+                device_id_type=MESH,
+            )
+
+        def begin(unit):
+            if direct:
+                exchange(unit, 0).start()
+
+        def finish(unit, phase):
+            exchange(unit, phase).wait_recv()
+            kept = piece(unit, phase, True)
+            come = arrived[phase][unit]
+            if phase + 1 < row_bits:
+                r.grads[kept] = r.grads[kept] + come
+                exchange(unit, phase + 1).start()
+                return
+            total = r.grads[kept].astype(FULL) + come.astype(FULL)
+            if unit < IN_UNIT:
+                spot = unit - OUT_UNIT
+                r.w_out_grad[spot * own_rows : (spot + 1) * own_rows, :] = total
+            elif unit < ATTN_UNIT:
+                spot = unit - IN_UNIT
+                r.w_in_grad[:, spot * half : (spot + 1) * half] = total
+            elif unit < QKV_UNIT:
+                r.w_attn_out_grad[...] = total
+            elif unit < UNITS - 1:
+                spot = unit - QKV_UNIT
+                r.w_query_key_grad[:, spot * half : (spot + 1) * half] = total
+            else:
+                r.w_value_grad[...] = total
+
+        events = sorted(
+            ((unit, phase) for unit in range(UNITS) for phase in range(4)),
+            key=lambda event: (event[0] // 3 + event[1], -event[1], event[0]),
+        )
+
+        def after_stage(stage):
+            if direct:
+                first = sum(AFTER_STAGE[:stage])
+                for event in events[first : first + AFTER_STAGE[stage]]:
+                    finish(*event)
+
+        def keep(unit, value):
+            value = value.astype(LOW)
+            r.grads[unit] = value.reshape(r.grads.shape[1:]) if direct else value
 
         lane = lax.broadcasted_iota(jnp.int32, (8, width), 1)
         doc_row = jnp.where(lane < r.doc_lengths[0], 0, 1)
@@ -142,23 +222,23 @@
         bias_upper, bias_lower = split(r.rel_bias[...])
         bias_last = (r.rel_bias[...] - bias_upper.astype(FULL) - bias_lower.astype(FULL)).astype(LOW)
         hot_low = hot.astype(LOW)
-        r.table[0:heads, :] = (
-            dot_tn(bias_upper, hot_low) + dot_tn(bias_lower, hot_low) + dot_tn(bias_last, hot_low)
-        )
-
-        r.small[...] = jnp.zeros_like(r.small)
+        r.table[0:heads, :] = dot(bias_upper, hot_low) + dot(bias_lower, hot_low) + dot(bias_last, hot_low)
+
+        r.small[0] = jnp.zeros((8, model + 2 * LANES), FULL)
         r.diagonals[...] = jnp.zeros_like(r.diagonals)
 
         inputs = r.tokens[...].astype(FULL)
-        normed = (inputs * inverse_root(inputs) * r.gain_attn[...]).astype(LOW)
+        normed = (inputs * inverse_root(inputs) * r.gain_attn[...][None]).astype(LOW)
         r.normed_one[0:width, :] = normed
-        w_query_key = weight("w_query_key")
+        loads[0].wait()
+        w_query_key = r.w_query_key_here
 
         @tiles(2 * model, TILE)
         def _(index, columns):
             r.qkv[:, columns] = dot(r.normed_one[0:width, :], w_query_key[:, columns]).astype(LOW)
 
-        w_value = weight("w_value")
+        loads[1].wait()
+        w_value = r.w_value_here
         r.qkv[:, 2 * model :] = dot(normed, w_value[...]).astype(LOW)
 
         pl.semaphore_wait(barrier, rows)
@@ -193,14 +273,16 @@
         r.mixed[0:width, :] = mixed
         send_mixed = to_partner(r.mixed.at[0:width], r.mixed.at[width : 2 * width], 1)
         send_mixed.start()
-        w_attn_out = weight("w_attn_out")
+        loads[2].wait()
+        w_attn_out = r.w_attn_out_here
         hidden = r.tokens[...].astype(FULL) + dot(mixed, w_attn_out[...])
         r.hidden_one[...] = hidden
-        r.normed_two[0:width, :] = (hidden * inverse_root(hidden) * r.gain_ff[...]).astype(LOW)
+        r.normed_two[0:width, :] = (hidden * inverse_root(hidden) * r.gain_ff[...][None]).astype(LOW)
         send_two = to_partner(r.normed_two.at[0:width], r.normed_two.at[width : 2 * width], 2)
         send_two.start()
 
-        w_in = weight("w_in")
+        loads[3].wait()
+        w_in = r.w_in_here
         bend = math.sqrt(2.0 / math.pi)
 
         @tiles(ff, TILE)
@@ -215,7 +297,8 @@
 
         send_active = to_partner(r.active.at[0:width], r.active.at[width : 2 * width], 3)
         send_active.start()
-        w_out = weight("w_out")
+        loads[4].wait()
+        w_out = r.w_out_here
 
         @tiles(model, model // 3)
         def _(index, columns):
@@ -224,7 +307,7 @@
             )
 
         hidden = r.hidden_two[...]
-        normed_upper, normed_lower = split(hidden * inverse_root(hidden) * r.gain_final[...])
+        normed_upper, normed_lower = split(hidden * inverse_root(hidden) * r.gain_final[...][None])
         member_low = member.astype(LOW)
         pooled = (dot(member_low, normed_upper) + dot(member_low, normed_lower)) * share
         pooled = pooled.astype(LOW).astype(FULL)
@@ -284,7 +367,8 @@
                 ]
             r.pooled[queries:, lanes] = r.pooled_docs[pl.ds(part, rows, stride=8), :]
 
-        w_proj = weight("w_proj")
+        loads[5].wait()
+        w_proj = r.w_proj_here
         pooled_low = r.pooled[...].astype(LOW)
         projected = dot(pooled_low, w_proj[...])
         scale = lax.rsqrt(jnp.sum(projected * projected, axis=-1, keepdims=True) + EPSILON)
@@ -294,8 +378,8 @@
         target = jnp.concatenate(
             [
                 (
-                    r.positives[:, query : query + 1]
-                    == lax.broadcasted_iota(jnp.int32, (rows, rows), 1)
+                    jnp.broadcast_to(r.positives[query : query + 1, :].astype(FULL), (rows, rows)).T
+                    == lax.broadcasted_iota(jnp.int32, (rows, rows), 1).astype(FULL)
                 ).astype(FULL)
                 for query in range(per_row)
             ],
@@ -334,8 +418,8 @@
             final_grad = jnp.where(seg_column == query, pooled_grad[query : query + 1, :], final_grad)
 
         hidden = r.hidden_two[...]
-        hidden_grad, r.small[2:3, :] = norm_backward(
-            hidden, inverse_root(hidden), r.gain_final[...], final_grad
+        hidden_grad, r.small[0, 2:3, 0:model] = norm_backward(
+            hidden, inverse_root(hidden), r.gain_final[...][None], final_grad
         )
         r.hidden_grad[...] = hidden_grad
         r.branch[...] = hidden_grad.astype(LOW)
@@ -347,6 +431,8 @@
 
         r.proj_grad_half[...] = r.proj_grad[:, own_half].astype(LOW)
         r.w_proj_whole[...] = dot_tn(r.pooled[...].astype(LOW), r.proj_grad_half[...])
+        if direct:
+            r.w_proj_grad[...] = r.w_proj_whole[pl.ds(pl.multiple_of(row * own_rows, 8), own_rows), :]
 
         @tiles(ff, TILE)
         def _(index, columns):
@@ -364,15 +450,29 @@
 
         @tiles(ff, model)
         def _(index, columns):
-            r.out_parts[index] = dot_tn(r.active[:, columns], r.branch_half[...]).astype(LOW)
+            value = dot_tn(r.active[:, columns], r.branch_half[...])
+            if direct:
+                per_tile = model * rows // ff
+                for unit in range(per_tile):
+                    for spot in range(per_tile):
+                        start = (spot * per_tile + unit) * own_rows
+                        r.grads[unit, index // 2, index % 2, spot // 2, spot % 2] = value[
+                            start : start + own_rows, :
+                        ].astype(LOW)
+            else:
+                keep(index, value)
+
+        for unit in range(OUT_UNIT, IN_UNIT):
+            begin(unit)
+        after_stage(0)
 
         @tiles(model, model // 3)
         def _(index, columns):
             r.normed_grad[:, columns] = dot_nt(r.inner_grad[...], w_in[columns, :])
 
         hidden = r.hidden_one[...]
-        through, r.small[1:2, :] = norm_backward(
-            hidden, inverse_root(hidden), r.gain_ff[...], r.normed_grad[...]
+        through, r.small[0, 1:2, 0:model] = norm_backward(
+            hidden, inverse_root(hidden), r.gain_ff[...][None], r.normed_grad[...]
         )
         hidden_grad = r.hidden_grad[...] + through
         r.hidden_grad[...] = hidden_grad
@@ -384,17 +484,23 @@
         send_two.wait()
         send_inner.wait()
 
-        @tiles(ff_half, TILE)
+        @tiles(ff_half, half)
         def _(index, columns):
-            r.in_parts[index] = dot_tn(r.normed_two[...], r.inner_half[:, columns]).astype(LOW)
+            keep(IN_UNIT + index, dot_tn(r.normed_two[...], r.inner_half[:, columns]))
+
+        for unit in range(IN_UNIT, ATTN_UNIT):
+            begin(unit)
+        after_stage(1)
 
         r.mixed_grad[...] = dot_nt(r.attn[...], w_attn_out[...]).astype(LOW)
         send_mixed.wait()
         send_attn.wait()
-        r.attn_parts[...] = dot_tn(r.mixed[...], r.attn_half[...]).astype(LOW)
-
-        @tiles(model, 2 * head_size)
-        def _(pair, columns):
+        keep(ATTN_UNIT, dot_tn(r.mixed[...], r.attn_half[...]))
+        begin(ATTN_UNIT)
+        after_stage(2)
+
+        def attention_back(pair):
+            columns = pl.ds(pl.multiple_of(pair * 2 * head_size, LANES), 2 * head_size)
             query = r.qkv[:, columns]
             value = r.qkv[:, pl.ds(pl.multiple_of(2 * model + pair * 2 * head_size, LANES), 2 * head_size)]
             mixed_grad = r.mixed_grad[:, columns]
@@ -429,6 +535,11 @@
                 jnp.where(after, value_sides[1], value_sides[0]).astype(LOW)
             )
 
+        pairs = heads // 2
+        lax.fori_loop(0, pairs // 2, lambda pair, carry: (attention_back(pair), carry)[1], 0)
+        after_stage(3)
+        lax.fori_loop(pairs // 2, pairs, lambda pair, carry: (attention_back(pair), carry)[1], 0)
+        after_stage(4)
         r.qkv_grad[:, 0:model] = r.queries_turned[...].T
 
         own_whole = pl.ds(pl.multiple_of(tower * model, LANES), model)
@@ -449,8 +560,8 @@
         normed_grad = dot_nt(r.qkv_grad[:, 0 : 2 * model], w_query_key[...])
         r.normed_grad[...] = normed_grad + dot_nt(r.qkv_grad[:, 2 * model :], w_value[...])
         inputs = r.tokens[...].astype(FULL)
-        through, r.small[0:1, :] = norm_backward(
-            inputs, inverse_root(inputs), r.gain_attn[...], r.normed_grad[...]
+        through, r.small[0, 0:1, 0:model] = norm_backward(
+            inputs, inverse_root(inputs), r.gain_attn[...][None], r.normed_grad[...]
         )
         r.tokens_grad[...] = r.hidden_grad[...] + through
 
@@ -460,31 +571,60 @@
             offsets = offsets + (pltpu.roll(row_lines, wide - line, 1) if line else row_lines)
         offset_upper, offset_lower = split(offsets)
         hot_low = r.hot[...]
-        r.small[8 : 8 + buckets, 0:16] = dot_nt(hot_low, offset_upper) + dot_nt(hot_low, offset_lower)
+        sums = dot_nt(offset_upper, hot_low) + dot_nt(offset_lower, hot_low)
+        r.small[0, 0:8, model : model + buckets] = sums[0:8]
+        r.small[0, 0:8, model + LANES : model + LANES + buckets] = sums[8:16]
 
         send_one.wait()
         send_qk.wait()
         send_value.wait()
-        r.qkv_parts[...] = dot_tn(r.normed_one[...], r.qkv_half[...]).astype(LOW)
-
-        small_rows = 8 + buckets
-        for bit in range(row_bits + 1):
+
+        @tiles(model + half, half)
+        def _(index, columns):
+            keep(QKV_UNIT + index, dot_tn(r.normed_one[...], r.qkv_half[:, columns]))
+
+        for unit in range(QKV_UNIT, UNITS):
+            begin(unit)
+        after_stage(5)
+
+        def small_begin(bit):
             peer = partner if bit == row_bits else (tower, jnp.bitwise_xor(row, 1 << bit))
-            copy = pltpu.make_async_remote_copy(
-                src_ref=r.small,
+            return pltpu.make_async_remote_copy(
+                src_ref=r.small.at[bit],
                 dst_ref=r.small_in.at[bit],
                 send_sem=r.small_send.at[bit],
                 recv_sem=r.small_recv.at[bit],
                 device_id=peer,
                 device_id_type=MESH,
             )
-            copy.start()
-            copy.wait()
-            r.small[...] = r.small[...] + r.small_in[bit]
-        r.gain_attn_grad[...] = r.small[0:1, :]
-        r.gain_ff_grad[...] = r.small[1:2, :]
-        r.gain_final_grad[...] = r.small[2:3, :]
-        r.rel_bias_grad[...] = r.small[8 : 8 + buckets, 0:heads]
+
+        def small_finish(bit):
+            small_begin(bit).wait_recv()
+            r.small[bit + 1] = r.small[bit] + r.small_in[bit]
+            if bit < row_bits:
+                small_begin(bit + 1).start()
+
+        small_begin(0).start()
+        if direct:
+            rest = events[sum(AFTER_STAGE) :]
+            for index, event in enumerate(rest):
+                finish(*event)
+                if index % 3 == 1 and index // 3 <= row_bits:
+                    small_finish(index // 3)
+            for unit in range(UNITS):
+                for phase in range(row_bits):
+                    exchange(unit, phase).wait_send()
+        else:
+            for bit in range(row_bits + 1):
+                small_finish(bit)
+        for bit in range(row_bits + 1):
+            small_begin(bit).wait_send()
+        total = row_bits + 1
+        r.gain_attn_grad[...] = r.small[total, 0, 0:model]
+        r.gain_ff_grad[...] = r.small[total, 1, 0:model]
+        r.gain_final_grad[...] = r.small[total, 2, 0:model]
+        r.rel_bias_grad[0:8, :] = r.small[total, 0:8, model : model + buckets]
+        r.rel_bias_grad[8:heads, :] = r.small[total, 0 : heads - 8, model + LANES : model + LANES + buckets]
 
     return kernel
 
@@ -519,127 +659,153 @@
         vmem = pl.BlockSpec(memory_space=pltpu.VMEM)
         smem = pl.BlockSpec(memory_space=pltpu.SMEM)
         hbm = pl.BlockSpec(memory_space=pl.ANY)
-        inputs = [
-            ("tokens", tokens[0], vmem),
-            ("query_segments", query_segments, vmem),
-            ("doc_lengths", doc_lengths, smem),
-            ("bucket_table", bucket_table[None], vmem),
-            ("positives", positives, vmem),
-            ("gain_attn", gain_attn[None], vmem),
-            ("w_query_key", w_query_key, hbm),
-            ("w_value", w_value, hbm),
-            ("w_attn_out", w_attn_out, hbm),
-            ("rel_bias", rel_bias, vmem),
-            ("gain_ff", gain_ff[None], vmem),
-            ("w_in", w_in, hbm),
-            ("w_out", w_out, hbm),
-            ("gain_final", gain_final[None], vmem),
-            ("w_proj", w_proj, hbm),
-        ]
-        outputs = [
-            ("loss", (1, 1), FULL),
-            ("tokens_grad", (width, model), FULL),
-            ("gain_attn_grad", (1, model), FULL),
-            ("gain_ff_grad", (1, model), FULL),
-            ("gain_final_grad", (1, model), FULL),
-            ("rel_bias_grad", (buckets, heads), FULL),
-            ("w_proj_whole", (model, half), FULL),
-            ("out_parts", (ff // model, model, half), LOW),
-            ("in_parts", (ff // 2 // TILE, model, TILE), LOW),
-            ("attn_parts", (model, half), LOW),
-            ("qkv_parts", (model, model + half), LOW),
-        ]
-        scratch = [
-            ("w_query_key_here", w_query_key.shape, LOW),
-            ("w_value_here", w_value.shape, LOW),
-            ("w_attn_out_here", w_attn_out.shape, LOW),
-            ("w_in_here", w_in.shape, LOW),
-            ("w_out_here", w_out.shape, LOW),
-            ("w_proj_here", w_proj.shape, LOW),
-            ("hot", (buckets, wide), LOW),
-            ("table", (16, wide), FULL),
-            ("allowed", (width, width), FULL),
-            ("normed_one", (2 * width, model), LOW),
-            ("qkv", (width, 3 * model), LOW),
-            ("keys_turned", (model, width), LOW),
-            ("values_turned", (model, width), LOW),
-            ("probs", (heads, width, width), LOW),
-            ("mixed_turned", (model, width), LOW),
-            ("mixed", (2 * width, model), LOW),
-            ("hidden_one", (width, model), FULL),
-            ("normed_two", (2 * width, model), LOW),
-            ("active", (2 * width, ff), LOW),
-            ("slope", (width, ff), LOW),
-            ("hidden_two", (width, model), FULL),
-            ("pooled_queries", (rows * per_row * model // LANES, LANES), FULL),
-            ("pooled_docs", (rows * 8, LANES), FULL),
-            ("pooled", (queries + rows, model), FULL),
-            ("proj_grad", (queries + rows, model), FULL),
-            ("proj_grad_half", (queries + rows, half), LOW),
-            ("own_grad", (16, model), FULL),
-            ("hidden_grad", (width, model), FULL),
-            ("branch", (width, model), LOW),
-            ("branch_half", (2 * width, half), LOW),
-            ("inner_grad", (width, ff), LOW),
-            ("inner_half", (2 * width, ff // 2), LOW),
-            ("normed_grad", (width, model), FULL),
-            ("attn", (width, model), LOW),
-            ("attn_half", (2 * width, half), LOW),
-            ("mixed_grad", (width, model), LOW),
-            ("score_grad", (width, width), FULL),
-            ("diagonals", (8, 16, wide), FULL),
-            ("queries_turned", (model, width), LOW),
-            ("qkv_grad", (width, 3 * model), LOW),
-            ("qkv_half", (2 * width, model + half), LOW),
-            ("small", (8 + buckets, model), FULL),
-            ("small_in", (row_bits + 1, 8 + buckets, model), FULL),
-        ]
-        semaphores = [
-            ("load_sem", 6),
-            ("core_send", 11),
-            ("core_recv", 11),
-            ("spread_send", rows),
-            ("spread_recv", rows),
-            ("small_send", row_bits + 1),
-            ("small_recv", row_bits + 1),
-        ]
-        names = [name for group in (inputs, outputs, scratch, semaphores) for name, *_ in group]
+        direct = in_kernel_sums(rows, model)
+        inputs = dict(
+            tokens=(tokens[0], vmem),
+            query_segments=(query_segments, vmem),
+            doc_lengths=(doc_lengths, smem),
+            bucket_table=(bucket_table[None], vmem),
+            positives=(positives.T, vmem),
+            gain_attn=(gain_attn, vmem),
+            w_query_key=(w_query_key, hbm),
+            w_value=(w_value, hbm),
+            w_attn_out=(w_attn_out, hbm),
+            rel_bias=(rel_bias.T, vmem),
+            gain_ff=(gain_ff, vmem),
+            w_in=(w_in, hbm),
+            w_out=(w_out, hbm),
+            gain_final=(gain_final, vmem),
+            w_proj=(w_proj, hbm),
+        )
+        outputs = dict(
+            loss=((1, 1), FULL),
+            tokens_grad=((width, model), FULL),
+            gain_attn_grad=((model,), FULL),
+            gain_ff_grad=((model,), FULL),
+            gain_final_grad=((model,), FULL),
+            rel_bias_grad=((heads, buckets), FULL),
+        )
+        whole = ((model, half), FULL)
+        if direct:
+            outputs.update(
+                w_query_key_grad=((own_rows, model), FULL),
+                w_value_grad=((own_rows, half), FULL),
+                w_attn_out_grad=((own_rows, half), FULL),
+                w_in_grad=((own_rows, ff // 2), FULL),
+                w_out_grad=((ff // rows, half), FULL),
+                w_proj_grad=((own_rows, half), FULL),
+            )
+            held = dict(
+                w_proj_whole=whole, grads=((UNITS,) + (2,) * row_bits + (own_rows, half), LOW)
+            )
+            arrived = [
+                pltpu.VMEM((UNITS,) + (2,) * (row_bits - 1 - phase) + (own_rows, half), LOW)
+                for phase in range(row_bits)
+            ]
+        else:
+            outputs.update(w_proj_whole=whole, grads=((UNITS, model, half), LOW))
+            held = {}
+            arrived = []
+        scratch = dict(
+            w_query_key_here=(w_query_key.shape, LOW),
+            w_value_here=(w_value.shape, LOW),
+            w_attn_out_here=(w_attn_out.shape, LOW),
+            w_in_here=(w_in.shape, LOW),
+            w_out_here=(w_out.shape, LOW),
+            w_proj_here=(w_proj.shape, LOW),
+            hot=((buckets, wide), LOW),
+            table=((16, wide), FULL),
+            allowed=((width, width), FULL),
+            normed_one=((2 * width, model), LOW),
+            qkv=((width, 3 * model), LOW),
+            keys_turned=((model, width), LOW),
+            values_turned=((model, width), LOW),
+            probs=((heads, width, width), LOW),
+            mixed_turned=((model, width), LOW),
+            mixed=((2 * width, model), LOW),
+            hidden_one=((width, model), FULL),
+            normed_two=((2 * width, model), LOW),
+            active=((2 * width, ff), LOW),
+            slope=((width, ff), LOW),
+            hidden_two=((width, model), FULL),
+            pooled_queries=((rows * per_row * model // LANES, LANES), FULL),
+            pooled_docs=((rows * 8, LANES), FULL),
+            pooled=((queries + rows, model), FULL),
+            proj_grad=((queries + rows, model), FULL),
+            proj_grad_half=((queries + rows, half), LOW),
+            own_grad=((16, model), FULL),
+            hidden_grad=((width, model), FULL),
+            branch=((width, model), LOW),
+            branch_half=((2 * width, half), LOW),
+            inner_grad=((width, ff), LOW),
+            inner_half=((2 * width, ff // 2), LOW),
+            normed_grad=((width, model), FULL),
+            attn=((width, model), LOW),
+            attn_half=((2 * width, half), LOW),
+            mixed_grad=((width, model), LOW),
+            score_grad=((width, width), FULL),
+            diagonals=((8, 16, wide), FULL),
+            queries_turned=((model, width), LOW),
+            qkv_grad=((width, 3 * model), LOW),
+            qkv_half=((2 * width, model + half), LOW),
+            small=((row_bits + 2, 8, model + 2 * LANES), FULL),
+            small_in=((row_bits + 1, 8, model + 2 * LANES), FULL),
+        )
+        scratch.update(held)
+        semaphores = dict(
+            load_sem=((6,)),
+            core_send=((11,)),
+            core_recv=((11,)),
+            spread_send=((rows,)),
+            spread_recv=((rows,)),
+            small_send=((row_bits + 1,)),
+            small_recv=((row_bits + 1,)),
+            sum_send=((UNITS, row_bits)),
+            sum_recv=((UNITS, row_bits)),
+        )
+        names = [*inputs, *outputs, *scratch, *semaphores]
         sizes = (rows, width, model, ff, heads, buckets, per_row)
         results = pl.pallas_call(
             make_kernel(sizes, names),
-            out_shape=[jax.ShapeDtypeStruct(shape, kind) for _, shape, kind in outputs],
-            in_specs=[spec for _, _, spec in inputs],
+            out_shape=[jax.ShapeDtypeStruct(shape, kind) for shape, kind in outputs.values()],
+            in_specs=[spec for _, spec in inputs.values()],
             out_specs=[vmem] * len(outputs),
-            scratch_shapes=[pltpu.VMEM(shape, kind) for _, shape, kind in scratch]
-            + [pltpu.SemaphoreType.DMA((count,)) for _, count in semaphores],
+            scratch_shapes=[pltpu.VMEM(shape, kind) for shape, kind in scratch.values()]
+            + [pltpu.SemaphoreType.DMA(shape) for shape in semaphores.values()]
+            + arrived,
             compiler_params=pltpu.CompilerParams(
                 collective_id=0, has_side_effects=True, vmem_limit_bytes=VMEM_LIMIT
             ),
-        )(*[array for _, array, _ in inputs])
-        r = dict(zip([name for name, *_ in outputs], results))
-
-        def over_rows(parts, axis):
-            return lax.psum_scatter(parts, "rows", scatter_dimension=axis, tiled=True).astype(FULL)
-
-        out_grad = over_rows(r["out_parts"].reshape(ff, half), 0)
-        in_grad = over_rows(r["in_parts"], 1).transpose(1, 0, 2).reshape(own_rows, ff // 2)
-        attn_grad = over_rows(r["attn_parts"], 0)
-        qkv_grad = over_rows(r["qkv_parts"], 0)
+        )(*[array for array, _ in inputs.values()])
+        r = SimpleNamespace(**dict(zip(outputs, results)))
+
+        if not direct:
+            rows_of = dict(scatter_dimension=0, tiled=True)
+            r.w_out_grad = lax.psum_scatter(
+                r.grads[:IN_UNIT].reshape(ff, half), "rows", **rows_of
+            ).astype(FULL)
+            others = r.grads[IN_UNIT:].transpose(1, 0, 2).reshape(model, -1)
+            others = lax.psum_scatter(others, "rows", **rows_of).astype(FULL)
+            r.w_in_grad = others[:, : ff // 2]
+            r.w_attn_out_grad = others[:, ff // 2 : ff // 2 + half]
+            r.w_query_key_grad = others[:, ff // 2 + half : ff // 2 + half + model]
+            r.w_value_grad = others[:, ff // 2 + half + model :]
+            r.w_proj_grad = lax.dynamic_slice_in_dim(
+                r.w_proj_whole, lax.axis_index("rows") * own_rows, own_rows, 0
+            )
         return (
-            r["loss"][0, 0],
-            r["tokens_grad"][None],
-            r["gain_attn_grad"][0],
-            qkv_grad[:, :model],
-            qkv_grad[:, model:],
-            attn_grad,
-            r["rel_bias_grad"],
-            r["gain_ff_grad"][0],
-            in_grad,
-            out_grad,
-            r["gain_final_grad"][0],
-            lax.dynamic_slice_in_dim(
-                r["w_proj_whole"], lax.axis_index("rows") * own_rows, own_rows, 0
-            ),
+            r.loss[0, 0],
+            r.tokens_grad[None],
+            r.gain_attn_grad,
+            r.w_query_key_grad,
+            r.w_value_grad,
+            r.w_attn_out_grad,
+            r.rel_bias_grad.T,
+            r.gain_ff_grad,
+            r.w_in_grad,
+            r.w_out_grad,
+            r.gain_final_grad,
+            r.w_proj_grad,
         )
 
     return step

time: 613 us -> 126 us (0.21)
  waiting for transfers between devices: 506 us -> 0 us
  Pallas kernels: 70.4 us -> 109 us
  between operations: 16.3 us -> 3.07 us
    reduce_scatter x4 -> x0, waiting for transfers between devices: 504 us -> none  [over_rows(): lax.psum_scatter(parts, 'rows', scatter_dimension=axis, tiled=True)]
    pallas_call x1, Pallas kernels: 70.4 us -> 109 us  [step(): pl.pallas_call(make_kernel(sizes, names), out_shape=[jax.ShapeDtypeStruct...]
    unnamed x14 -> x19, local copies, waits for them, and re-layouts: 4.41 us -> 13.2 us
  transfers between devices with their start and end apart: 4 -> 0, of which waited for: 4 -> 0; matrix products, arithmetic and copies ran while one was open for 2% -> 0% of each run, Pallas kernels for 0% -> 0%
where the time goes in v2:
time: 126 us
  Pallas kernels  109 us (87%)
  local copies, waits for them, and re-layouts  13.2 us (10%)
  between operations  3.07 us (2%)
    pallas_call x1, Pallas kernels, step(): pl.pallas_call(make_kernel(sizes, names), out_shape=[jax.ShapeDtypeStruct...  109 us
    unnamed x19, local copies, waits for them, and re-layouts  13.2 us

profile of v2, /device:TPU:0, one launch (start us, length us, event | category | flops | bytes accessed | tf_op | source)
XLA Modules:
  0.0 125.6 jit_solution(6885463365217509971)
XLA Ops:
  1.3 109.3 %shard_map.238 = (f32[1,1]{1,0:T(1,128)}, f32[256,768]{1,0:T(8,128)}, f32[768]{0:T(1024)}, f32[768]{0:T(1024)}, f32[768]{0:T(1024)}, /*index=5*/f32[12,32]{1,0:T...) custom-call(bf16[256,768]{1,0:T(8,128)(2,1)} %bitcast.8, ...), custom_call_target="tpu_custom_call" | custom-call | tf_op jit(solution)/shard_map/pallas_call | solution.py:768
  110.6 0.0 copy-start.1
  110.6 0.0 copy-start
  110.6 0.0 copy-start.3
  110.7 0.0 copy-start.2
  111.3 2.1 %copy.41 = f32[1,256,768]{2,1,0:T(8,128)} copy(f32[1,256,768]{2,1,0:T(8,128)} %bitcast.7) | data formatting | bytes 1572864
  113.3 1.3 %copy.42 = f32[768]{0:T(1024)} copy(f32[768]{0:T(1024)} %get-tuple-element.50) | data formatting | bytes 6144
  114.6 1.6 %copy.43 = f32[48,768]{1,0:T(8,128)} copy(f32[48,768]{1,0:T(8,128)} %get-tuple-element.51) | data formatting | bytes 294912
  116.2 1.5 %copy.44 = f32[48,384]{1,0:T(8,128)} copy(f32[48,384]{1,0:T(8,128)} %get-tuple-element.52) | data formatting | bytes 147456
  117.7 1.5 %copy.45 = f32[48,384]{1,0:T(8,128)} copy(f32[48,384]{1,0:T(8,128)} %get-tuple-element.53) | data formatting | bytes 147456
  119.2 1.3 %copy.46 = f32[32,12]{0,1:T(8,128)} copy(f32[32,12]{0,1:T(8,128)} %bitcast.10) | data formatting | bytes 3072
  120.5 1.3 %copy.47 = f32[768]{0:T(1024)} copy(f32[768]{0:T(1024)} %get-tuple-element.55) | data formatting | bytes 6144
  121.8 0.0 copy-done.1
  121.8 0.7 copy.48
  122.5 0.0 copy-done
  122.5 0.7 copy.49
  123.2 0.0 copy-done.3
  123.2 0.6 copy.50
  123.8 0.0 copy-done.2
  123.8 0.6 copy.51
Async XLA Ops:
  110.6 11.2 %copy-start.1 = (f32[48,1536]{1,0:T(8,128)S(1)}, f32[48,1536]{1,0:T(8,128)}, u32[]{:S(2)}) copy-start(f32[48,1536]{1,0:T(8,128)} %get-tuple-element.56) | copy-start | bytes 884740
  110.6 11.9 %copy-start = (f32[192,384]{1,0:T(8,128)S(1)}, f32[192,384]{1,0:T(8,128)}, u32[]{:S(2)}) copy-start(f32[192,384]{1,0:T(8,128)} %get-tuple-element.57) | copy-start | bytes 884740
  110.6 12.6 %copy-start.3 = (f32[768]{0:T(1024)S(1)}, f32[768]{0:T(1024)}, u32[]{:S(2)}) copy-start(f32[768]{0:T(1024)} %get-tuple-element.58) | copy-start | bytes 9220
  110.7 13.2 %copy-start.2 = (f32[48,384]{1,0:T(8,128)S(1)}, f32[48,384]{1,0:T(8,128)}, u32[]{:S(2)}) copy-start(f32[48,384]{1,0:T(8,128)} %get-tuple-element.59) | copy-start | bytes 221188

commit v3 on v2

--- a/solution.py
+++ b/solution.py
@@ -19,15 +19,18 @@
 VMEM_LIMIT = 60 * 2**20
 
 Z_HALF, Z_PAIR, Y, X = range(4)
-X_FIRST = (X, Y, Z_PAIR, Z_HALF)
-Y_FIRST = (Y, X, Z_PAIR, Z_HALF)
-Z_THEN_X = (Z_PAIR, X, Y, Z_HALF)
-Z_THEN_Y = (Z_PAIR, Y, X, Z_HALF)
+X_FIRST = ((X,), (Y,), (Z_PAIR, Z_HALF))
+Y_FIRST = ((Y,), (X,), (Z_PAIR, Z_HALF))
+Z_THEN_X = ((Z_PAIR,), (X,), (Y, Z_HALF))
+Z_THEN_Y = ((Z_PAIR,), (Y,), (X, Z_HALF))
 ORDERS = (
     X_FIRST, Y_FIRST, Z_THEN_X, X_FIRST, Y_FIRST, Z_THEN_Y,
     X_FIRST, Y_FIRST, Z_THEN_X, X_FIRST, Y_FIRST, Z_THEN_Y,
 )
-AFTER_STAGE = (0, 0, 3, 3, 3, 3)
+BITS = 4
+STEPS = 3
+AFTER_STAGE = (0, 1, 3, 4, 4, 3)
+STAGGER = 4
 OUT_UNIT, IN_UNIT, ATTN_UNIT, QKV_UNIT, UNITS = 0, 4, 8, 9, 12
 
 
@@ -71,7 +74,7 @@
 
 
 def in_kernel_sums(rows, model):
-    return rows == 2 ** len(ORDERS[0]) and model % (16 * rows) == 0
+    return rows == 2**BITS and model % (16 * rows) == 0
 
 
 def make_kernel(sizes, names):
@@ -130,40 +133,63 @@
                 device_id_type=MESH,
             )
 
-        coordinate = [jnp.bitwise_and(lax.shift_right_logical(row, 3 - bit), 1) for bit in range(4)]
-
-        def piece(unit, phase, kept):
-            order = ORDERS[unit]
-            place = [slice(None)] * 4
-            for bit in order[:phase]:
-                place[bit] = coordinate[bit]
-            last = order[phase]
-            place[last] = coordinate[last] if kept else 1 - coordinate[last]
-            return (unit, *place)
-
-        def exchange(unit, phase):
+        coordinate = [jnp.bitwise_and(lax.shift_right_logical(row, 3 - bit), 1) for bit in range(BITS)]
+
+        def piece(unit, step, code):
+            place = [slice(None)] * BITS
+            for bits in ORDERS[unit][:step]:
+                for bit in bits:
+                    place[bit] = coordinate[bit]
+            for spot, bit in enumerate(ORDERS[unit][step]):
+                place[bit] = jnp.bitwise_xor(coordinate[bit], (code >> spot) & 1)
+            return place
+
+        def exchange(unit, step, code=1, half=None):
+            place = piece(unit, step, code)
+            into = arrived[step].at[unit]
+            index = step + code - 1
+            if step == STEPS - 1:
+                into = into.at[code - 1]
+            elif half is not None:
+                place[Z_PAIR] = jnp.bitwise_xor(coordinate[Z_PAIR], 1 - half)
+                into = into.at[:, place[Z_PAIR]]
+                index = STEPS + 2 + half
+            peer = row
+            for spot, bit in enumerate(ORDERS[unit][step]):
+                peer = jnp.bitwise_xor(peer, ((code >> spot) & 1) << (3 - bit))
             return pltpu.make_async_remote_copy(
-                src_ref=r.grads.at[piece(unit, phase, False)],
-                dst_ref=arrived[phase].at[unit],
-                send_sem=r.sum_send.at[unit, phase],
-                recv_sem=r.sum_recv.at[unit, phase],
-                device_id=(tower, jnp.bitwise_xor(row, 1 << (3 - ORDERS[unit][phase]))),
+                src_ref=r.grads.at[(unit, *place)],
+                dst_ref=into,
+                send_sem=r.sum_send.at[unit, index],
+                recv_sem=r.sum_recv.at[unit, index],
+                device_id=(tower, peer),
                 device_id_type=MESH,
             )
 
+        def exchanges(unit, step):
+            if step == STEPS - 1:
+                return [exchange(unit, step, code) for code in (1, 2, 3)]
+            if step == 0 and unit < IN_UNIT and Z_PAIR not in ORDERS[unit][0]:
+                return [exchange(unit, step, 1, half) for half in range(2)]
+            return [exchange(unit, step)]
+
         def begin(unit):
             if direct:
-                exchange(unit, 0).start()
-
-        def finish(unit, phase):
-            exchange(unit, phase).wait_recv()
-            kept = piece(unit, phase, True)
-            come = arrived[phase][unit]
-            if phase + 1 < row_bits:
-                r.grads[kept] = r.grads[kept] + come
-                exchange(unit, phase + 1).start()
+                for copy in exchanges(unit, 0):
+                    copy.start()
+
+        def finish(unit, step):
+            for copy in exchanges(unit, step):
+                copy.wait_recv()
+            kept = (unit, *piece(unit, step, 0))
+            if step + 1 < STEPS:
+                r.grads[kept] = r.grads[kept] + arrived[step][unit]
+                for copy in exchanges(unit, step + 1):
+                    copy.start()
                 return
-            total = r.grads[kept].astype(FULL) + come.astype(FULL)
+            total = r.grads[kept].astype(FULL)
+            for other in range(3):
+                total = total + arrived[step][unit, other].astype(FULL)
             if unit < IN_UNIT:
                 spot = unit - OUT_UNIT
                 r.w_out_grad[spot * own_rows : (spot + 1) * own_rows, :] = total
@@ -179,8 +205,8 @@
                 r.w_value_grad[...] = total
 
         events = sorted(
-            ((unit, phase) for unit in range(UNITS) for phase in range(4)),
-            key=lambda event: (event[0] // 3 + event[1], -event[1], event[0]),
+            ((unit, step) for unit in range(UNITS) for step in range(STEPS)),
+            key=lambda event: (event[0] + STAGGER * event[1], -event[1]),
         )
 
         def after_stage(stage):
@@ -240,10 +266,6 @@
         loads[1].wait()
         w_value = r.w_value_here
         r.qkv[:, 2 * model :] = dot(normed, w_value[...]).astype(LOW)
-
-        pl.semaphore_wait(barrier, rows)
-        send_one = to_partner(r.normed_one.at[0:width], r.normed_one.at[width : 2 * width], 0)
-        send_one.start()
 
         r.keys_turned[...] = r.qkv[:, model : 2 * model].T
         r.values_turned[...] = r.qkv[:, 2 * model :].T
@@ -271,6 +293,9 @@
 
         mixed = r.mixed_turned[...].T
         r.mixed[0:width, :] = mixed
+        pl.semaphore_wait(barrier, rows)
+        send_one = to_partner(r.normed_one.at[0:width], r.normed_one.at[width : 2 * width], 0)
+        send_one.start()
         send_mixed = to_partner(r.mixed.at[0:width], r.mixed.at[width : 2 * width], 1)
         send_mixed.start()
         loads[2].wait()
@@ -300,13 +325,8 @@
         loads[4].wait()
         w_out = r.w_out_here
 
-        @tiles(model, model // 3)
-        def _(index, columns):
-            r.hidden_two[:, columns] = r.hidden_one[:, columns] + dot(
-                r.active[0:width, :], w_out[:, columns]
-            )
-
-        hidden = r.hidden_two[...]
+        hidden = r.hidden_one[...] + dot(r.active[0:width, :], w_out[...])
+        r.hidden_two[...] = hidden
         normed_upper, normed_lower = split(hidden * inverse_root(hidden) * r.gain_final[...][None])
         member_low = member.astype(LOW)
         pooled = (dot(member_low, normed_upper) + dot(member_low, normed_lower)) * share
@@ -434,6 +454,37 @@
         if direct:
             r.w_proj_grad[...] = r.w_proj_whole[pl.ds(pl.multiple_of(row * own_rows, 8), own_rows), :]
 
+        send_active.wait()
+        send_branch.wait()
+        per_tile = model * rows // ff
+        if direct:
+            for half_step in range(2):
+                pair = jnp.bitwise_xor(coordinate[Z_PAIR], 1 - half_step)
+
+                def tile(half_z, carry):
+                    columns = pl.ds(pl.multiple_of((2 * half_z + pair) * model, model), model)
+                    value = dot_tn(r.active[:, columns], r.branch_half[...])
+                    for unit in range(per_tile):
+                        for spot in range(per_tile):
+                            start = (spot * per_tile + unit) * own_rows
+                            r.grads[unit, half_z, pair, spot // 2, spot % 2] = value[
+                                start : start + own_rows, :
+                            ].astype(LOW)
+                    return carry
+
+                lax.fori_loop(0, 2, tile, 0)
+                for unit in range(OUT_UNIT, IN_UNIT):
+                    sends = exchanges(unit, 0)
+                    if half_step < len(sends):
+                        sends[half_step].start()
+        else:
+
+            @tiles(ff, model)
+            def _(index, columns):
+                keep(index, dot_tn(r.active[:, columns], r.branch_half[...]))
+
+        after_stage(0)
+
         @tiles(ff, TILE)
         def _(index, columns):
             active_grad = dot_nt(r.branch[...], w_out[columns, :])
@@ -445,31 +496,7 @@
         send_inner.start()
         r.inner_half[0:width, :] = r.inner_grad[:, own_ff]
 
-        send_active.wait()
-        send_branch.wait()
-
-        @tiles(ff, model)
-        def _(index, columns):
-            value = dot_tn(r.active[:, columns], r.branch_half[...])
-            if direct:
-                per_tile = model * rows // ff
-                for unit in range(per_tile):
-                    for spot in range(per_tile):
-                        start = (spot * per_tile + unit) * own_rows
-                        r.grads[unit, index // 2, index % 2, spot // 2, spot % 2] = value[
-                            start : start + own_rows, :
-                        ].astype(LOW)
-            else:
-                keep(index, value)
-
-        for unit in range(OUT_UNIT, IN_UNIT):
-            begin(unit)
-        after_stage(0)
-
-        @tiles(model, model // 3)
-        def _(index, columns):
-            r.normed_grad[:, columns] = dot_nt(r.inner_grad[...], w_in[columns, :])
-
+        r.normed_grad[...] = dot_nt(r.inner_grad[...], w_in[...])
         hidden = r.hidden_one[...]
         through, r.small[0, 1:2, 0:model] = norm_backward(
             hidden, inverse_root(hidden), r.gain_ff[...][None], r.normed_grad[...]
@@ -612,8 +639,9 @@
                 if index % 3 == 1 and index // 3 <= row_bits:
                     small_finish(index // 3)
             for unit in range(UNITS):
-                for phase in range(row_bits):
-                    exchange(unit, phase).wait_send()
+                for step in range(STEPS):
+                    for copy in exchanges(unit, step):
+                        copy.wait_send()
         else:
             for bit in range(row_bits + 1):
                 small_finish(bit)
@@ -627,6 +655,19 @@
         r.rel_bias_grad[8:heads, :] = r.small[total, 0 : heads - 8, model + LANES : model + LANES + buckets]
 
     return kernel
+
+
+def copy_out(*args):
+    *arrays, sems = args
+    count = len(arrays) // 2
+    copies = [
+        pltpu.make_async_copy(arrays[index], arrays[count + index], sems.at[index])
+        for index in range(count)
+    ]
+    for copy in copies:
+        copy.start()
+    for copy in copies:
+        copy.wait()
 
 
 def on_device(rows):
@@ -699,8 +740,7 @@
                 w_proj_whole=whole, grads=((UNITS,) + (2,) * row_bits + (own_rows, half), LOW)
             )
             arrived = [
-                pltpu.VMEM((UNITS,) + (2,) * (row_bits - 1 - phase) + (own_rows, half), LOW)
-                for phase in range(row_bits)
+                pltpu.VMEM((UNITS, *count, own_rows, half), LOW) for count in ((2, 2, 2), (2, 2), (3,))
             ]
         else:
             outputs.update(w_proj_whole=whole, grads=((UNITS, model, half), LOW))
@@ -760,8 +800,8 @@
             spread_recv=((rows,)),
             small_send=((row_bits + 1,)),
             small_recv=((row_bits + 1,)),
-            sum_send=((UNITS, row_bits)),
-            sum_recv=((UNITS, row_bits)),
+            sum_send=((UNITS, STEPS + 4)),
+            sum_recv=((UNITS, STEPS + 4)),
         )
         names = [*inputs, *outputs, *scratch, *semaphores]
         sizes = (rows, width, model, ff, heads, buckets, per_row)
@@ -777,6 +817,14 @@
                 collective_id=0, has_side_effects=True, vmem_limit_bytes=VMEM_LIMIT
             ),
         )(*[array for array, _ in inputs.values()])
+        if direct:
+            results = pl.pallas_call(
+                copy_out,
+                out_shape=[jax.ShapeDtypeStruct(shape, kind) for shape, kind in outputs.values()],
+                in_specs=[vmem] * len(outputs),
+                out_specs=[hbm] * len(outputs),
+                scratch_shapes=[pltpu.SemaphoreType.DMA((len(outputs),))],
+            )(*results)
         r = SimpleNamespace(**dict(zip(outputs, results)))
 
         if not direct:

time: 126 us -> 107 us (0.85)
  local copies, waits for them, and re-layouts: 13.2 us -> 0 us
  Pallas kernels: 109 us -> 106 us
  between operations: 3.07 us -> 1.46 us
    unnamed x19 -> x0, local copies, waits for them, and re-layouts: 13.2 us -> none
    pallas_call x1, Pallas kernels: 109 us -> 102 us  [step(): pl.pallas_call(make_kernel(sizes, names), out_shape=[jax.ShapeDtypeStruct...]
    pallas_call x0 -> x1, Pallas kernels: none -> 3.47 us  [step(): pl.pallas_call(copy_out, out_shape=[jax.ShapeDtypeStruct(shape, kind) for...]
where the time goes in v3:
time: 107 us
  Pallas kernels  106 us (99%)
  between operations  1.46 us (1%)
    pallas_call x1, Pallas kernels, step(): pl.pallas_call(make_kernel(sizes, names), out_shape=[jax.ShapeDtypeStruct...  102 us
    pallas_call x1, Pallas kernels, step(): pl.pallas_call(copy_out, out_shape=[jax.ShapeDtypeStruct(shape, kind) for...  3.47 us

profile of v3, /device:TPU:0, one launch (start us, length us, event | category | flops | bytes accessed | tf_op | source)
XLA Modules:
  0.0 107.0 jit_solution(14610985222020755156)
XLA Ops:
  1.3 102.1 %shard_map.238 = (f32[1,1]{1,0:T(1,128)}, f32[256,768]{1,0:T(8,128)}, f32[768]{0:T(1024)}, f32[768]{0:T(1024)}, f32[768]{0:T(1024)}, /*index=5*/f32[12,32]{1,0:T...) custom-call(bf16[256,768]{1,0:T(8,128)(2,1)} %bitcast.7, ...), custom_call_target="tpu_custom_call" | custom-call | tf_op jit(solution)/shard_map/pallas_call | solution.py:808
  103.4 3.5 %shard_map.239 = (f32[1,1]{1,0:T(1,128)}, f32[256,768]{1,0:T(8,128)}, f32[768]{0:T(1024)}, f32[768]{0:T(1024)}, f32[768]{0:T(1024)}, /*index=5*/f32[12,32]{1,0:T...) custom-call(f32[1,1]{1,0:T(1,128)} %get-tuple-element.36.args_0_, ...), custom_call_target="tpu_custom_call" | custom-call | tf_op jit(solution)/shard_map/pallas_call | solution.py:821

commit v4 on v3

--- a/solution.py
+++ b/solution.py
@@ -1,3 +1,4 @@
+import functools
 import math
 from types import SimpleNamespace
 
@@ -19,19 +20,52 @@
 VMEM_LIMIT = 60 * 2**20
 
 Z_HALF, Z_PAIR, Y, X = range(4)
-X_FIRST = ((X,), (Y,), (Z_PAIR, Z_HALF))
-Y_FIRST = ((Y,), (X,), (Z_PAIR, Z_HALF))
-Z_THEN_X = ((Z_PAIR,), (X,), (Y, Z_HALF))
-Z_THEN_Y = ((Z_PAIR,), (Y,), (X, Z_HALF))
 ORDERS = (
-    X_FIRST, Y_FIRST, Z_THEN_X, X_FIRST, Y_FIRST, Z_THEN_Y,
-    X_FIRST, Y_FIRST, Z_THEN_X, X_FIRST, Y_FIRST, Z_THEN_Y,
+    ((X,), (Y,), (Z_PAIR, Z_HALF)),
+    ((Y,), (X,), (Z_PAIR, Z_HALF)),
+    ((X, Y), (Z_PAIR,), (Z_HALF,)),
+    ((Z_PAIR,), (Y,), (X,), (Z_HALF,)),
+    ((Z_PAIR,), (X,), (Y,), (Z_HALF,)),
+    ((X,), (Y,), (Z_PAIR, Z_HALF)),
+    ((Z_PAIR,), (Y,), (X, Z_HALF)),
+    ((Z_PAIR,), (X,), (Y,), (Z_HALF,)),
+    ((Y,), (X,), (Z_PAIR, Z_HALF)),
+    ((X,), (Y,), (Z_PAIR, Z_HALF)),
+    ((Z_PAIR,), (X,), (Y,), (Z_HALF,)),
+    ((Y,), (X,), (Z_PAIR, Z_HALF)),
+)
+PLAN = (
+    (),
+    (),
+    (),
+    (),
+    (),
+    (),
+    (),
+    (),
+    (),
+    (),
+    ((3, 0),),
+    (),
+    (),
+    ((0, 0), (1, 0),),
+    (),
+    (),
+    ((2, 0),),
+    (),
+    ((4, 0), (3, 1),),
+    (),
+    (),
+    ((0, 1), (5, 0),),
+    (),
+    ((6, 0),),
+    ((1, 1),),
+    ((8, 0), (4, 1),),
+    ((3, 2), (7, 0), (5, 1), (2, 1), (12, 0), (0, 2), (6, 1), (9, 0), (12, 1), (8, 1), (12, 2), (10, 0), (11, 0), (4, 2), (7, 1), (1, 2), (3, 3), (12, 3), (9, 1), (5, 2), (2, 2), (10, 1), (7, 2), (12, 4), (6, 2), (11, 1), (8, 2), (4, 3), (10, 2), (9, 2), (7, 3), (11, 2), (10, 3),),
 )
 BITS = 4
-STEPS = 3
-AFTER_STAGE = (0, 1, 3, 4, 4, 3)
-STAGGER = 4
 OUT_UNIT, IN_UNIT, ATTN_UNIT, QKV_UNIT, UNITS = 0, 4, 8, 9, 12
+SMALL = UNITS
 
 
 def dot(left, right):
@@ -77,8 +111,8 @@
     return rows == 2**BITS and model % (16 * rows) == 0
 
 
-def make_kernel(sizes, names):
-    rows, width, model, ff, heads, buckets, per_row = sizes
+def make_kernel(sizes, names, small_inputs):
+    rows, width, model, ff, heads, buckets, per_row, count_in, count_out = sizes
     head_size = model // heads
     half = model // 2
     ff_half = ff // 2
@@ -90,7 +124,34 @@
 
     def kernel(*args):
         r = SimpleNamespace(**dict(zip(names, args)))
-        arrived = args[len(names) :]
+        extra = args[len(names) :]
+        near_inputs, extra = extra[: len(small_inputs)], extra[len(small_inputs) :]
+        far_inputs = [getattr(r, name) for name in small_inputs]
+        r.__dict__.update(zip(small_inputs, near_inputs))
+        far_results = args[count_in : count_in + count_out]
+        near_results = extra[:count_out]
+        leaving = []
+        if direct:
+            r.__dict__.update(zip(names[count_in : count_in + count_out], near_results))
+
+        def publish(result):
+            if direct:
+                index = next(index for index, ref in enumerate(near_results) if ref is result)
+                copy = pltpu.make_async_copy(result, far_results[index], r.leave_sem.at[index])
+                copy.start()
+                leaving.append(copy)
+
+        parts_left = [4, 4, 1, 2, 1]
+
+        def finished(group, result):
+            parts_left[group] -= 1
+            if not parts_left[group]:
+                publish(result)
+
+        landing = []
+        if direct:
+            landings = iter(extra[count_out:])
+            landing = [[next(landings) for _ in steps] for steps in ORDERS]
         tower = lax.axis_index("tower")
         row = lax.axis_index("rows")
         partner = (1 - tower, row)
@@ -117,11 +178,23 @@
                     (r.w_in, r.w_in_here),
                     (r.w_out, r.w_out_here),
                     (r.w_proj, r.w_proj_here),
+                    *zip(far_inputs, near_inputs),
                 )
             )
         ]
-        for load in loads:
-            load.start()
+
+        def load(index):
+            loads[index].start()
+
+        def loaded(index):
+            loads[index].wait()
+
+        for index in range(6, len(loads)):
+            load(index)
+        for index in range(6):
+            load(index)
+        for index in range(6, len(loads)):
+            loaded(index)
 
         def to_partner(src, dst, index):
             return pltpu.make_async_remote_copy(
@@ -144,34 +217,41 @@
                 place[bit] = jnp.bitwise_xor(coordinate[bit], (code >> spot) & 1)
             return place
 
-        def exchange(unit, step, code=1, half=None):
+        def exchange(unit, step, code, half=None):
             place = piece(unit, step, code)
-            into = arrived[step].at[unit]
-            index = step + code - 1
-            if step == STEPS - 1:
+            into = landing[unit][step]
+            if len(ORDERS[unit][step]) > 1:
                 into = into.at[code - 1]
             elif half is not None:
                 place[Z_PAIR] = jnp.bitwise_xor(coordinate[Z_PAIR], 1 - half)
                 into = into.at[:, place[Z_PAIR]]
-                index = STEPS + 2 + half
             peer = row
             for spot, bit in enumerate(ORDERS[unit][step]):
                 peer = jnp.bitwise_xor(peer, ((code >> spot) & 1) << (3 - bit))
             return pltpu.make_async_remote_copy(
                 src_ref=r.grads.at[(unit, *place)],
                 dst_ref=into,
-                send_sem=r.sum_send.at[unit, index],
-                recv_sem=r.sum_recv.at[unit, index],
+                send_sem=r.sum_send.at[unit],
+                recv_sem=r.sum_recv.at[unit, step],
                 device_id=(tower, peer),
                 device_id_type=MESH,
             )
 
         def exchanges(unit, step):
-            if step == STEPS - 1:
-                return [exchange(unit, step, code) for code in (1, 2, 3)]
-            if step == 0 and unit < IN_UNIT and Z_PAIR not in ORDERS[unit][0]:
+            bits = ORDERS[unit][step]
+            if step == 0 and unit < IN_UNIT and bits[0] in (X, Y) and len(bits) == 1:
                 return [exchange(unit, step, 1, half) for half in range(2)]
-            return [exchange(unit, step)]
+            return [exchange(unit, step, code) for code in range(1, 2 ** len(bits))]
+
+        def all_of(ref, send_sem, recv_sem):
+            return pltpu.make_async_remote_copy(
+                src_ref=ref,
+                dst_ref=ref,
+                send_sem=send_sem,
+                recv_sem=recv_sem,
+                device_id=partner,
+                device_id_type=MESH,
+            )
 
         def begin(unit):
             if direct:
@@ -179,41 +259,65 @@
                     copy.start()
 
         def finish(unit, step):
-            for copy in exchanges(unit, step):
-                copy.wait_recv()
+            if unit == SMALL:
+                small_finish(step)
+                return
+            all_of(landing[unit][step], r.sum_send.at[unit], r.sum_recv.at[unit, step]).wait_recv()
             kept = (unit, *piece(unit, step, 0))
-            if step + 1 < STEPS:
-                r.grads[kept] = r.grads[kept] + arrived[step][unit]
+            come = landing[unit][step]
+            several = len(ORDERS[unit][step]) > 1
+            if step + 1 < len(ORDERS[unit]):
+                if several:
+                    total = r.grads[kept].astype(FULL)
+                    for other in range(3):
+                        total = total + come[other].astype(FULL)
+                    r.grads[kept] = total.astype(LOW)
+                else:
+                    r.grads[kept] = r.grads[kept] + come[...]
                 for copy in exchanges(unit, step + 1):
                     copy.start()
                 return
             total = r.grads[kept].astype(FULL)
-            for other in range(3):
-                total = total + arrived[step][unit, other].astype(FULL)
+            if several:
+                for other in range(3):
+                    total = total + come[other].astype(FULL)
+            else:
+                total = total + come[...].astype(FULL)
             if unit < IN_UNIT:
                 spot = unit - OUT_UNIT
                 r.w_out_grad[spot * own_rows : (spot + 1) * own_rows, :] = total
+                finished(0, r.w_out_grad)
             elif unit < ATTN_UNIT:
                 spot = unit - IN_UNIT
                 r.w_in_grad[:, spot * half : (spot + 1) * half] = total
+                finished(1, r.w_in_grad)
             elif unit < QKV_UNIT:
                 r.w_attn_out_grad[...] = total
+                finished(2, r.w_attn_out_grad)
             elif unit < UNITS - 1:
                 spot = unit - QKV_UNIT
                 r.w_query_key_grad[:, spot * half : (spot + 1) * half] = total
+                finished(3, r.w_query_key_grad)
             else:
                 r.w_value_grad[...] = total
-
-        events = sorted(
-            ((unit, step) for unit in range(UNITS) for step in range(STEPS)),
-            key=lambda event: (event[0] + STAGGER * event[1], -event[1]),
-        )
-
-        def after_stage(stage):
-            if direct:
-                first = sum(AFTER_STAGE[:stage])
-                for event in events[first : first + AFTER_STAGE[stage]]:
-                    finish(*event)
+                finished(4, r.w_value_grad)
+
+        def small_exchange(step):
+            peer = partner if step == row_bits else (tower, jnp.bitwise_xor(row, 1 << step))
+            return pltpu.make_async_remote_copy(
+                src_ref=r.small.at[step],
+                dst_ref=r.small_in.at[step],
+                send_sem=r.small_send.at[0],
+                recv_sem=r.small_recv.at[step],
+                device_id=peer,
+                device_id_type=MESH,
+            )
+
+        def small_finish(step):
+            small_exchange(step).wait_recv()
+            r.small[step + 1] = r.small[step] + r.small_in[step]
+            if step < row_bits:
+                small_exchange(step + 1).start()
 
         def keep(unit, value):
             value = value.astype(LOW)
@@ -250,46 +354,58 @@
         hot_low = hot.astype(LOW)
         r.table[0:heads, :] = dot(bias_upper, hot_low) + dot(bias_lower, hot_low) + dot(bias_last, hot_low)
 
+        allowed = seg_column == seg_row[0:1]
+
+        def spread_bias(head, carry):
+            line = jnp.broadcast_to(r.table[pl.ds(head, 1), :], (width, wide))
+            bias = pltpu.roll(line, width + 1, 1, stride=1, stride_axis=0)[:, :width]
+            r.bias[head] = jnp.where(allowed, bias, MASKED)
+            return carry
+
+        lax.fori_loop(0, heads, spread_bias, 0)
         r.small[0] = jnp.zeros((8, model + 2 * LANES), FULL)
         r.diagonals[...] = jnp.zeros_like(r.diagonals)
 
         inputs = r.tokens[...].astype(FULL)
         normed = (inputs * inverse_root(inputs) * r.gain_attn[...][None]).astype(LOW)
         r.normed_one[0:width, :] = normed
-        loads[0].wait()
+        loaded(0)
         w_query_key = r.w_query_key_here
 
-        @tiles(2 * model, TILE)
-        def _(index, columns):
-            r.qkv[:, columns] = dot(r.normed_one[0:width, :], w_query_key[:, columns]).astype(LOW)
-
-        loads[1].wait()
+        for start in range(0, 2 * model, TILE):
+            columns = slice(start, start + TILE)
+            r.qkv[:, columns] = dot(normed, w_query_key[:, columns]).astype(LOW)
+
+        loaded(1)
         w_value = r.w_value_here
         r.qkv[:, 2 * model :] = dot(normed, w_value[...]).astype(LOW)
 
         r.keys_turned[...] = r.qkv[:, model : 2 * model].T
         r.values_turned[...] = r.qkv[:, 2 * model :].T
 
-        allowed = seg_column == seg_row[0:1]
-        r.allowed[...] = allowed.astype(FULL)
-
-        @tiles(model, 2 * head_size)
-        def _(pair, columns):
-            query = r.qkv[:, columns]
-            key = r.qkv[:, pl.ds(pl.multiple_of(model + pair * 2 * head_size, LANES), 2 * head_size)]
-            place = lax.broadcasted_iota(jnp.int32, (width, 2 * head_size), 1)
+        place = lax.broadcasted_iota(jnp.int32, (width, 2 * head_size), 1)
+
+        def attend(pair):
+            start = pair * 2 * head_size
+            query = r.qkv[:, start : start + 2 * head_size]
+            key = r.qkv[:, model + start : model + start + 2 * head_size]
             for side in range(2):
                 head = 2 * pair + side
                 own = (place >= head_size) if side else (place < head_size)
-                score = dot_nt(jnp.where(own, key, jnp.zeros_like(key)), query)
-                line = jnp.broadcast_to(r.table[pl.ds(head, 1), :], (width, wide))
-                bias = pltpu.roll(line, width + 1, 1, stride=1, stride_axis=0)[:, :width]
-                score = jnp.where(r.allowed[...] > 0.5, score + bias, MASKED)
+                score = dot_nt(jnp.where(own, key, jnp.zeros_like(key)), query) + r.bias[head]
                 weights = jnp.exp(score - jnp.max(score, axis=0, keepdims=True))
-                prob = (weights * (1.0 / jnp.sum(weights, axis=0, keepdims=True))).astype(LOW)
-                r.probs[head] = prob
-                here = pl.ds(pl.multiple_of(head * head_size, head_size), head_size)
-                r.mixed_turned[here, :] = dot(r.values_turned[here, :], prob).astype(LOW)
+                r.probs[head] = (weights * (1.0 / jnp.sum(weights, axis=0, keepdims=True))).astype(LOW)
+
+        def mix(pair):
+            for head in (2 * pair, 2 * pair + 1):
+                here = slice(head * head_size, (head + 1) * head_size)
+                r.mixed_turned[here, :] = dot(r.values_turned[here, :], r.probs[head]).astype(LOW)
+
+        for pair in range(heads // 2):
+            attend(pair)
+            if pair:
+                mix(pair - 1)
+        mix(heads // 2 - 1)
 
         mixed = r.mixed_turned[...].T
         r.mixed[0:width, :] = mixed
@@ -298,31 +414,29 @@
         send_one.start()
         send_mixed = to_partner(r.mixed.at[0:width], r.mixed.at[width : 2 * width], 1)
         send_mixed.start()
-        loads[2].wait()
+        loaded(2)
         w_attn_out = r.w_attn_out_here
         hidden = r.tokens[...].astype(FULL) + dot(mixed, w_attn_out[...])
         r.hidden_one[...] = hidden
-        r.normed_two[0:width, :] = (hidden * inverse_root(hidden) * r.gain_ff[...][None]).astype(LOW)
+        normed_two = (hidden * inverse_root(hidden) * r.gain_ff[...][None]).astype(LOW)
+        r.normed_two[0:width, :] = normed_two
         send_two = to_partner(r.normed_two.at[0:width], r.normed_two.at[width : 2 * width], 2)
         send_two.start()
 
-        loads[3].wait()
+        loaded(3)
         w_in = r.w_in_here
         bend = math.sqrt(2.0 / math.pi)
 
-        @tiles(ff, TILE)
-        def _(index, columns):
-            inner = dot(r.normed_two[0:width, :], w_in[:, columns])
-            square = inner * inner
-            curve = jnp.tanh(bend * (inner * (1.0 + 0.044715 * square)))
-            lift = 0.5 * (1.0 + curve)
-            r.active[0:width, columns] = (inner * lift).astype(LOW)
-            slope = 0.5 * inner * (1.0 - curve * curve) * (bend * (1.0 + 3 * 0.044715 * square))
-            r.slope[:, columns] = (lift + slope).astype(LOW)
+        for start in range(0, ff, TILE):
+            columns = slice(start, start + TILE)
+            inner = dot(normed_two, w_in[:, columns])
+            curve = jnp.tanh(inner * (bend + (bend * 0.044715) * (inner * inner)))
+            r.inner[:, columns] = inner
+            r.active[0:width, columns] = (inner * (0.5 + 0.5 * curve)).astype(LOW)
 
         send_active = to_partner(r.active.at[0:width], r.active.at[width : 2 * width], 3)
         send_active.start()
-        loads[4].wait()
+        loaded(4)
         w_out = r.w_out_here
 
         hidden = r.hidden_one[...] + dot(r.active[0:width, :], w_out[...])
@@ -335,21 +449,20 @@
         own_queries = r.pooled_queries.at[pl.ds(pl.multiple_of(row * query_message, 8), query_message)]
         own_doc = r.pooled_docs.at[pl.ds(pl.multiple_of(row * 8, 8), 8)]
 
-        def spread(block, act):
-            def step(index, carry):
-                act(
-                    pltpu.make_async_remote_copy(
-                        src_ref=block,
-                        dst_ref=block,
-                        send_sem=r.spread_send.at[index],
-                        recv_sem=r.spread_recv.at[index],
-                        device_id=(tower, jnp.bitwise_xor(row, index)),
-                        device_id_type=MESH,
-                    )
-                )
-                return carry
-
-            lax.fori_loop(1, rows, step, 0)
+        def spread(block, whole):
+            for index in range(1, rows):
+                pltpu.make_async_remote_copy(
+                    src_ref=block,
+                    dst_ref=block,
+                    send_sem=r.spread_sem.at[0],
+                    recv_sem=r.spread_sem.at[1],
+                    device_id=(tower, jnp.bitwise_xor(row, rows - index)),
+                    device_id_type=MESH,
+                ).start()
+            others = whole.at[0 : whole.shape[0] // rows * (rows - 1)]
+            every = all_of(others, r.spread_sem.at[0], r.spread_sem.at[1])
+            every.wait_send()
+            every.wait_recv()
 
         relay_queries = to_partner(r.pooled_queries, r.pooled_queries, 4)
         relay_docs = to_partner(r.pooled_docs, r.pooled_docs, 5)
@@ -361,8 +474,7 @@
                 r.pooled_queries[pl.ds(spot, per_row), :] = pooled[
                     0:per_row, part * LANES : (part + 1) * LANES
                 ]
-            spread(own_queries, lambda copy: copy.start())
-            spread(own_queries, lambda copy: copy.wait())
+            spread(own_queries, r.pooled_queries)
             relay_queries.start()
             relay_docs.wait_recv()
             relay_queries.wait_send()
@@ -373,8 +485,7 @@
             for part in range(parts):
                 spot = pl.multiple_of(row * 8, 8) + part
                 r.pooled_docs[pl.ds(spot, 1), :] = pooled[0:1, part * LANES : (part + 1) * LANES]
-            spread(own_doc, lambda copy: copy.start())
-            spread(own_doc, lambda copy: copy.wait())
+            spread(own_doc, r.pooled_docs)
             relay_docs.start()
             relay_queries.wait_recv()
             relay_docs.wait_send()
@@ -387,7 +498,7 @@
                 ]
             r.pooled[queries:, lanes] = r.pooled_docs[pl.ds(part, rows, stride=8), :]
 
-        loads[5].wait()
+        loaded(5)
         w_proj = r.w_proj_here
         pooled_low = r.pooled[...].astype(LOW)
         projected = dot(pooled_low, w_proj[...])
@@ -409,6 +520,7 @@
         log_sum = highest + jnp.log(jnp.sum(jnp.exp(logits - highest), axis=-1, keepdims=True))
         missed = log_sum - jnp.sum(logits * target, axis=-1, keepdims=True)
         r.loss[...] = jnp.sum(missed, axis=0, keepdims=True) / queries
+        publish(r.loss)
         logits_grad = (jnp.exp(logits - log_sum) - target) * (LOGIT_SCALE / queries)
         grad_upper, grad_lower = split(logits_grad)
         embed_grad = jnp.concatenate(
@@ -453,6 +565,7 @@
         r.w_proj_whole[...] = dot_tn(r.pooled[...].astype(LOW), r.proj_grad_half[...])
         if direct:
             r.w_proj_grad[...] = r.w_proj_whole[pl.ds(pl.multiple_of(row * own_rows, 8), own_rows), :]
+            publish(r.w_proj_grad)
 
         send_active.wait()
         send_branch.wait()
@@ -461,7 +574,7 @@
             for half_step in range(2):
                 pair = jnp.bitwise_xor(coordinate[Z_PAIR], 1 - half_step)
 
-                def tile(half_z, carry):
+                def tile(half_z):
                     columns = pl.ds(pl.multiple_of((2 * half_z + pair) * model, model), model)
                     value = dot_tn(r.active[:, columns], r.branch_half[...])
                     for unit in range(per_tile):
@@ -470,61 +583,83 @@
                             r.grads[unit, half_z, pair, spot // 2, spot % 2] = value[
                                 start : start + own_rows, :
                             ].astype(LOW)
-                    return carry
-
-                lax.fori_loop(0, 2, tile, 0)
+
+                for half_z in range(2):
+                    tile(half_z)
                 for unit in range(OUT_UNIT, IN_UNIT):
                     sends = exchanges(unit, 0)
-                    if half_step < len(sends):
+                    if len(sends) == 2:
                         sends[half_step].start()
+                    elif half_step == (Z_PAIR not in ORDERS[unit][0]):
+                        for copy in sends:
+                            copy.start()
         else:
 
             @tiles(ff, model)
             def _(index, columns):
                 keep(index, dot_tn(r.active[:, columns], r.branch_half[...]))
 
-        after_stage(0)
-
-        @tiles(ff, TILE)
-        def _(index, columns):
+        pieces = []
+
+        def then(body):
+            pieces.append(body)
+            return body
+
+        def inner_back(index):
+            columns = pl.ds(index * TILE, TILE)
             active_grad = dot_nt(r.branch[...], w_out[columns, :])
-            r.inner_grad[:, columns] = (active_grad * r.slope[:, columns].astype(FULL)).astype(LOW)
+            inner = r.inner[:, columns]
+            square = inner * inner
+            curve = jnp.tanh(inner * (bend + (bend * 0.044715) * square))
+            slope = (0.5 * inner) * (1.0 - curve * curve) * (bend + (bend * 3 * 0.044715) * square)
+            r.inner_grad[:, columns] = (active_grad * ((0.5 + 0.5 * curve) + slope)).astype(LOW)
+
+        for index in range(ff // TILE):
+            then(functools.partial(inner_back, index))
 
         own_ff = pl.ds(pl.multiple_of(tower * ff_half, LANES), ff_half)
         other_ff = pl.ds(pl.multiple_of((1 - tower) * ff_half, LANES), ff_half)
         send_inner = to_partner(r.inner_grad.at[:, other_ff], r.inner_half.at[width : 2 * width], 7)
-        send_inner.start()
-        r.inner_half[0:width, :] = r.inner_grad[:, own_ff]
-
-        r.normed_grad[...] = dot_nt(r.inner_grad[...], w_in[...])
-        hidden = r.hidden_one[...]
-        through, r.small[0, 1:2, 0:model] = norm_backward(
-            hidden, inverse_root(hidden), r.gain_ff[...][None], r.normed_grad[...]
-        )
-        hidden_grad = r.hidden_grad[...] + through
-        r.hidden_grad[...] = hidden_grad
-        r.attn[...] = hidden_grad.astype(LOW)
         send_attn = to_partner(r.attn.at[:, other_half], r.attn_half.at[width : 2 * width], 8)
-        send_attn.start()
-        r.attn_half[0:width, :] = r.attn[:, own_half]
-
-        send_two.wait()
-        send_inner.wait()
-
-        @tiles(ff_half, half)
-        def _(index, columns):
+
+        @then
+        def _():
+            send_inner.start()
+            r.inner_half[0:width, :] = r.inner_grad[:, own_ff]
+            r.normed_grad[...] = dot_nt(r.inner_grad[...], w_in[...])
+
+        @then
+        def _():
+            hidden = r.hidden_one[...]
+            through, r.small[0, 1:2, 0:model] = norm_backward(
+                hidden, inverse_root(hidden), r.gain_ff[...][None], r.normed_grad[...]
+            )
+            hidden_grad = r.hidden_grad[...] + through
+            r.hidden_grad[...] = hidden_grad
+            r.attn[...] = hidden_grad.astype(LOW)
+            send_attn.start()
+            r.attn_half[0:width, :] = r.attn[:, own_half]
+            send_two.wait()
+            send_inner.wait()
+
+        def in_grad(index):
+            columns = pl.ds(index * half, half)
             keep(IN_UNIT + index, dot_tn(r.normed_two[...], r.inner_half[:, columns]))
-
-        for unit in range(IN_UNIT, ATTN_UNIT):
-            begin(unit)
-        after_stage(1)
-
-        r.mixed_grad[...] = dot_nt(r.attn[...], w_attn_out[...]).astype(LOW)
-        send_mixed.wait()
-        send_attn.wait()
-        keep(ATTN_UNIT, dot_tn(r.mixed[...], r.attn_half[...]))
-        begin(ATTN_UNIT)
-        after_stage(2)
+            begin(IN_UNIT + index)
+
+        for index in range(ATTN_UNIT - IN_UNIT):
+            then(functools.partial(in_grad, index))
+
+        @then
+        def _():
+            r.mixed_grad[...] = dot_nt(r.attn[...], w_attn_out[...]).astype(LOW)
+
+        @then
+        def _():
+            send_mixed.wait()
+            send_attn.wait()
+            keep(ATTN_UNIT, dot_tn(r.mixed[...], r.attn_half[...]))
+            begin(ATTN_UNIT)
 
         def attention_back(pair):
             columns = pl.ds(pl.multiple_of(pair * 2 * head_size, LANES), 2 * head_size)
@@ -562,12 +697,8 @@
                 jnp.where(after, value_sides[1], value_sides[0]).astype(LOW)
             )
 
-        pairs = heads // 2
-        lax.fori_loop(0, pairs // 2, lambda pair, carry: (attention_back(pair), carry)[1], 0)
-        after_stage(3)
-        lax.fori_loop(pairs // 2, pairs, lambda pair, carry: (attention_back(pair), carry)[1], 0)
-        after_stage(4)
-        r.qkv_grad[:, 0:model] = r.queries_turned[...].T
+        for pair in range(heads // 2):
+            then(functools.partial(attention_back, pair))
 
         own_whole = pl.ds(pl.multiple_of(tower * model, LANES), model)
         other_whole = pl.ds(pl.multiple_of((1 - tower) * model, LANES), model)
@@ -579,95 +710,97 @@
         send_value = to_partner(
             r.qkv_grad.at[:, other_value], r.qkv_half.at[width : 2 * width, model:], 10
         )
-        send_qk.start()
-        send_value.start()
-        r.qkv_half[0:width, 0:model] = r.qkv_grad[:, own_whole]
-        r.qkv_half[0:width, model:] = r.qkv_grad[:, own_value]
-
-        normed_grad = dot_nt(r.qkv_grad[:, 0 : 2 * model], w_query_key[...])
-        r.normed_grad[...] = normed_grad + dot_nt(r.qkv_grad[:, 2 * model :], w_value[...])
-        inputs = r.tokens[...].astype(FULL)
-        through, r.small[0, 0:1, 0:model] = norm_backward(
-            inputs, inverse_root(inputs), r.gain_attn[...][None], r.normed_grad[...]
-        )
-        r.tokens_grad[...] = r.hidden_grad[...] + through
-
-        offsets = jnp.zeros((16, wide), FULL)
-        for line in range(8):
-            row_lines = r.diagonals[line]
-            offsets = offsets + (pltpu.roll(row_lines, wide - line, 1) if line else row_lines)
-        offset_upper, offset_lower = split(offsets)
-        hot_low = r.hot[...]
-        sums = dot_nt(offset_upper, hot_low) + dot_nt(offset_lower, hot_low)
-        r.small[0, 0:8, model : model + buckets] = sums[0:8]
-        r.small[0, 0:8, model + LANES : model + LANES + buckets] = sums[8:16]
-
-        send_one.wait()
-        send_qk.wait()
-        send_value.wait()
-
-        @tiles(model + half, half)
-        def _(index, columns):
+
+        @then
+        def _():
+            r.qkv_grad[:, 0:model] = r.queries_turned[...].T
+            send_qk.start()
+            send_value.start()
+            r.qkv_half[0:width, 0:model] = r.qkv_grad[:, own_whole]
+            r.qkv_half[0:width, model:] = r.qkv_grad[:, own_value]
+            send_one.wait()
+            send_qk.wait()
+            send_value.wait()
+
+        def qkv_back(index):
+            columns = pl.ds(index * half, half)
             keep(QKV_UNIT + index, dot_tn(r.normed_one[...], r.qkv_half[:, columns]))
-
-        for unit in range(QKV_UNIT, UNITS):
-            begin(unit)
-        after_stage(5)
-
-        def small_begin(bit):
-            peer = partner if bit == row_bits else (tower, jnp.bitwise_xor(row, 1 << bit))
-            return pltpu.make_async_remote_copy(
-                src_ref=r.small.at[bit],
-                dst_ref=r.small_in.at[bit],
-                send_sem=r.small_send.at[bit],
-                recv_sem=r.small_recv.at[bit],
-                device_id=peer,
-                device_id_type=MESH,
-            )
-
-        def small_finish(bit):
-            small_begin(bit).wait_recv()
-            r.small[bit + 1] = r.small[bit] + r.small_in[bit]
-            if bit < row_bits:
-                small_begin(bit + 1).start()
-
-        small_begin(0).start()
-        if direct:
-            rest = events[sum(AFTER_STAGE) :]
-            for index, event in enumerate(rest):
-                finish(*event)
-                if index % 3 == 1 and index // 3 <= row_bits:
-                    small_finish(index // 3)
-            for unit in range(UNITS):
-                for step in range(STEPS):
-                    for copy in exchanges(unit, step):
-                        copy.wait_send()
-        else:
-            for bit in range(row_bits + 1):
-                small_finish(bit)
-        for bit in range(row_bits + 1):
-            small_begin(bit).wait_send()
+            begin(QKV_UNIT + index)
+
+        for index in range(UNITS - QKV_UNIT):
+            then(functools.partial(qkv_back, index))
+
+        @then
+        def _():
+            normed_grad = dot_nt(r.qkv_grad[:, 0 : 2 * model], w_query_key[...])
+            r.normed_grad[...] = normed_grad + dot_nt(r.qkv_grad[:, 2 * model :], w_value[...])
+
+        @then
+        def _():
+            inputs = r.tokens[...].astype(FULL)
+            through, r.small[0, 0:1, 0:model] = norm_backward(
+                inputs, inverse_root(inputs), r.gain_attn[...][None], r.normed_grad[...]
+            )
+            r.tokens_grad[...] = r.hidden_grad[...] + through
+            publish(r.tokens_grad)
+
+            offsets = jnp.zeros((16, wide), FULL)
+            for line in range(8):
+                row_lines = r.diagonals[line]
+                offsets = offsets + (pltpu.roll(row_lines, wide - line, 1) if line else row_lines)
+            offset_upper, offset_lower = split(offsets)
+            hot_low = r.hot[...]
+            sums = dot_nt(offset_upper, hot_low) + dot_nt(offset_lower, hot_low)
+            r.small[0, 0:8, model : model + buckets] = sums[0:8]
+            r.small[0, 0:8, model + LANES : model + LANES + buckets] = sums[8:16]
+            small_exchange(0).start()
+
+        for index in range(len(pieces) + 1):
+            if index:
+                pieces[index - 1]()
+            if direct:
+                for event in PLAN[index]:
+                    finish(*event)
+
+        if not direct:
+            for step in range(row_bits + 1):
+                small_finish(step)
         total = row_bits + 1
         r.gain_attn_grad[...] = r.small[total, 0, 0:model]
         r.gain_ff_grad[...] = r.small[total, 1, 0:model]
         r.gain_final_grad[...] = r.small[total, 2, 0:model]
         r.rel_bias_grad[0:8, :] = r.small[total, 0:8, model : model + buckets]
         r.rel_bias_grad[8:heads, :] = r.small[total, 0 : heads - 8, model + LANES : model + LANES + buckets]
+        for result in (r.gain_attn_grad, r.gain_ff_grad, r.gain_final_grad, r.rel_bias_grad):
+            publish(result)
+        if direct:
+            sent = r.w_proj_whole.at[0 : (rows - 1) * own_rows // 2]
+            for unit in range(UNITS):
+                all_of(sent, r.sum_send.at[unit], r.sum_recv.at[unit, 0]).wait_send()
+        all_of(r.small_in, r.small_send.at[0], r.small_recv.at[0]).wait_send()
+        for copy in leaving:
+            copy.wait()
 
     return kernel
 
 
 def copy_out(*args):
-    *arrays, sems = args
-    count = len(arrays) // 2
-    copies = [
-        pltpu.make_async_copy(arrays[index], arrays[count + index], sems.at[index])
+    count = (len(args) - 2) // 3
+    here = args[2 * count : 3 * count]
+    ways = [
+        (
+            pltpu.make_async_copy(args[index], here[index], args[-2].at[index]),
+            pltpu.make_async_copy(here[index], args[count + index], args[-1].at[index]),
+        )
         for index in range(count)
     ]
-    for copy in copies:
-        copy.start()
-    for copy in copies:
-        copy.wait()
+    for come, _ in ways:
+        come.start()
+    for come, leave in ways:
+        come.wait()
+        leave.start()
+    for _, leave in ways:
+        leave.wait()
 
 
 def on_device(rows):
@@ -698,25 +831,24 @@
         row_bits = rows.bit_length() - 1
         own_rows = model // rows
         vmem = pl.BlockSpec(memory_space=pltpu.VMEM)
-        smem = pl.BlockSpec(memory_space=pltpu.SMEM)
         hbm = pl.BlockSpec(memory_space=pl.ANY)
         direct = in_kernel_sums(rows, model)
         inputs = dict(
-            tokens=(tokens[0], vmem),
-            query_segments=(query_segments, vmem),
-            doc_lengths=(doc_lengths, smem),
-            bucket_table=(bucket_table[None], vmem),
-            positives=(positives.T, vmem),
-            gain_attn=(gain_attn, vmem),
-            w_query_key=(w_query_key, hbm),
-            w_value=(w_value, hbm),
-            w_attn_out=(w_attn_out, hbm),
-            rel_bias=(rel_bias.T, vmem),
-            gain_ff=(gain_ff, vmem),
-            w_in=(w_in, hbm),
-            w_out=(w_out, hbm),
-            gain_final=(gain_final, vmem),
-            w_proj=(w_proj, hbm),
+            tokens=(tokens[0], pltpu.VMEM),
+            query_segments=(query_segments, pltpu.VMEM),
+            doc_lengths=(doc_lengths, pltpu.SMEM),
+            bucket_table=(bucket_table[None], pltpu.VMEM),
+            positives=(positives.T, pltpu.VMEM),
+            gain_attn=(gain_attn, pltpu.VMEM),
+            w_query_key=(w_query_key, None),
+            w_value=(w_value, None),
+            w_attn_out=(w_attn_out, None),
+            rel_bias=(rel_bias.T, pltpu.VMEM),
+            gain_ff=(gain_ff, pltpu.VMEM),
+            w_in=(w_in, None),
+            w_out=(w_out, None),
+            gain_final=(gain_final, pltpu.VMEM),
+            w_proj=(w_proj, None),
         )
         outputs = dict(
             loss=((1, 1), FULL),
@@ -739,9 +871,13 @@
             held = dict(
                 w_proj_whole=whole, grads=((UNITS,) + (2,) * row_bits + (own_rows, half), LOW)
             )
-            arrived = [
-                pltpu.VMEM((UNITS, *count, own_rows, half), LOW) for count in ((2, 2, 2), (2, 2), (3,))
-            ]
+            arrived = []
+            for steps in ORDERS:
+                left = BITS
+                for bits in steps:
+                    left -= len(bits)
+                    several = (3,) if len(bits) > 1 else ()
+                    arrived.append(pltpu.VMEM(several + (2,) * left + (own_rows, half), LOW))
         else:
             outputs.update(w_proj_whole=whole, grads=((UNITS, model, half), LOW))
             held = {}
@@ -755,7 +891,7 @@
             w_proj_here=(w_proj.shape, LOW),
             hot=((buckets, wide), LOW),
             table=((16, wide), FULL),
-            allowed=((width, width), FULL),
+            bias=((heads, width, width), FULL),
             normed_one=((2 * width, model), LOW),
             qkv=((width, 3 * model), LOW),
             keys_turned=((model, width), LOW),
@@ -766,7 +902,7 @@
             hidden_one=((width, model), FULL),
             normed_two=((2 * width, model), LOW),
             active=((2 * width, ff), LOW),
-            slope=((width, ff), LOW),
+            inner=((width, ff), FULL),
             hidden_two=((width, model), FULL),
             pooled_queries=((rows * per_row * model // LANES, LANES), FULL),
             pooled_docs=((rows * 8, LANES), FULL),
@@ -793,25 +929,29 @@
         )
         scratch.update(held)
         semaphores = dict(
-            load_sem=((6,)),
+            load_sem=((len(inputs),)),
             core_send=((11,)),
             core_recv=((11,)),
-            spread_send=((rows,)),
-            spread_recv=((rows,)),
-            small_send=((row_bits + 1,)),
+            spread_sem=((2,)),
+            small_send=((1,)),
             small_recv=((row_bits + 1,)),
-            sum_send=((UNITS, STEPS + 4)),
-            sum_recv=((UNITS, STEPS + 4)),
+            sum_send=((UNITS,)),
+            leave_sem=(len(outputs),),
+            sum_recv=((UNITS, BITS)),
         )
         names = [*inputs, *outputs, *scratch, *semaphores]
-        sizes = (rows, width, model, ff, heads, buckets, per_row)
+        small_inputs = [name for name, (_, place) in inputs.items() if place is not None]
+        nears = [pltpu.VMEM(shape, kind) for shape, kind in outputs.values()] if direct else []
+        sizes = (rows, width, model, ff, heads, buckets, per_row, len(inputs), len(outputs))
         results = pl.pallas_call(
-            make_kernel(sizes, names),
+            make_kernel(sizes, names, small_inputs),
             out_shape=[jax.ShapeDtypeStruct(shape, kind) for shape, kind in outputs.values()],
-            in_specs=[spec for _, spec in inputs.values()],
-            out_specs=[vmem] * len(outputs),
+            in_specs=[hbm] * len(inputs),
+            out_specs=[hbm if direct else vmem] * len(outputs),
             scratch_shapes=[pltpu.VMEM(shape, kind) for shape, kind in scratch.values()]
             + [pltpu.SemaphoreType.DMA(shape) for shape in semaphores.values()]
+            + [inputs[name][1](inputs[name][0].shape, inputs[name][0].dtype) for name in small_inputs]
+            + nears
             + arrived,
             compiler_params=pltpu.CompilerParams(
                 collective_id=0, has_side_effects=True, vmem_limit_bytes=VMEM_LIMIT
@@ -821,9 +961,9 @@
             results = pl.pallas_call(
                 copy_out,
                 out_shape=[jax.ShapeDtypeStruct(shape, kind) for shape, kind in outputs.values()],
-                in_specs=[vmem] * len(outputs),
+                in_specs=[hbm] * len(outputs),
                 out_specs=[hbm] * len(outputs),
-                scratch_shapes=[pltpu.SemaphoreType.DMA((len(outputs),))],
+                scratch_shapes=nears + [pltpu.SemaphoreType.DMA((len(outputs),))] * 2,
             )(*results)
         r = SimpleNamespace(**dict(zip(outputs, results)))
 

time: 107 us -> 94.8 us (0.89)
  Pallas kernels: 106 us -> 93.2 us
    pallas_call x1, Pallas kernels: 102 us -> 89.9 us  [step(): pl.pallas_call(make_kernel(sizes, names, small_inputs), out_shape=[jax.Sh...]
where the time goes in v4:
time: 94.8 us; the launch traced here: 94.6 us
  Pallas kernels  93.2 us (98%)
  between operations  1.48 us (2%)
    pallas_call x1, Pallas kernels, step(): pl.pallas_call(make_kernel(sizes, names, small_inputs), out_shape=[jax.Sh...  89.9 us
    pallas_call x1, Pallas kernels, step(): pl.pallas_call(copy_out, out_shape=[jax.ShapeDtypeStruct(shape, kind) for...  3.24 us

profile of v4, /device:TPU:0, one launch (start us, length us, event | category | flops | bytes accessed | tf_op | source)
XLA Modules:
  0.0 94.6 jit_solution(11274810378347075178)
XLA Ops:
  1.3 89.9 %shard_map.238 = (f32[1,1]{1,0:T(1,128)}, f32[256,768]{1,0:T(8,128)}, f32[768]{0:T(1024)}, f32[768]{0:T(1024)}, f32[768]{0:T(1024)}, /*index=5*/f32[12,32]{1,0:T...) custom-call(bf16[256,768]{1,0:T(8,128)(2,1)} %bitcast.7, ...), custom_call_target="tpu_custom_call" | custom-call | tf_op jit(solution)/shard_map/pallas_call | solution.py:946
  91.2 3.2 %shard_map.239 = (f32[1,1]{1,0:T(1,128)}, f32[256,768]{1,0:T(8,128)}, f32[768]{0:T(1024)}, f32[768]{0:T(1024)}, f32[768]{0:T(1024)}, /*index=5*/f32[12,32]{1,0:T...) custom-call(f32[1,1]{1,0:T(1,128)} %get-tuple-element.36.args_0_, ...), custom_call_target="tpu_custom_call" | custom-call | tf_op jit(solution)/shard_map/pallas_call | solution.py:961

commit v5 on v4

--- a/solution.py
+++ b/solution.py
@@ -22,17 +22,17 @@
 Z_HALF, Z_PAIR, Y, X = range(4)
 ORDERS = (
     ((X,), (Y,), (Z_PAIR, Z_HALF)),
-    ((Y,), (X,), (Z_PAIR, Z_HALF)),
-    ((X, Y), (Z_PAIR,), (Z_HALF,)),
-    ((Z_PAIR,), (Y,), (X,), (Z_HALF,)),
+    ((Y,), (X,), (Z_PAIR,), (Z_HALF,)),
+    ((Z_PAIR,), (Y,), (Z_HALF,), (X,)),
+    ((Z_PAIR,), (Y,), (Z_HALF,), (X,)),
+    ((X,), (Y,), (Z_PAIR, Z_HALF)),
+    ((Y,), (X,), (Z_PAIR,), (Z_HALF,)),
     ((Z_PAIR,), (X,), (Y,), (Z_HALF,)),
-    ((X,), (Y,), (Z_PAIR, Z_HALF)),
+    ((X,), (Z_PAIR,), (Y,), (Z_HALF,)),
     ((Z_PAIR,), (Y,), (X, Z_HALF)),
-    ((Z_PAIR,), (X,), (Y,), (Z_HALF,)),
-    ((Y,), (X,), (Z_PAIR, Z_HALF)),
-    ((X,), (Y,), (Z_PAIR, Z_HALF)),
-    ((Z_PAIR,), (X,), (Y,), (Z_HALF,)),
-    ((Y,), (X,), (Z_PAIR, Z_HALF)),
+    ((X,), (Y,), (Z_PAIR,), (Z_HALF,)),
+    ((X,), (Y,), (Z_PAIR,), (Z_HALF,)),
+    ((Y,), (X,), (Z_PAIR,), (Z_HALF,)),
 )
 PLAN = (
     (),
@@ -45,23 +45,24 @@
     (),
     (),
     (),
-    ((3, 0),),
-    (),
-    (),
-    ((0, 0), (1, 0),),
-    (),
-    (),
-    ((2, 0),),
-    (),
-    ((4, 0), (3, 1),),
-    (),
-    (),
-    ((0, 1), (5, 0),),
-    (),
-    ((6, 0),),
-    ((1, 1),),
-    ((8, 0), (4, 1),),
-    ((3, 2), (7, 0), (5, 1), (2, 1), (12, 0), (0, 2), (6, 1), (9, 0), (12, 1), (8, 1), (12, 2), (10, 0), (11, 0), (4, 2), (7, 1), (1, 2), (3, 3), (12, 3), (9, 1), (5, 2), (2, 2), (10, 1), (7, 2), (12, 4), (6, 2), (11, 1), (8, 2), (4, 3), (10, 2), (9, 2), (7, 3), (11, 2), (10, 3),),
+    (),
+    (),
+    ((0, 0), (1, 0), (2, 0),),
+    (),
+    (),
+    (),
+    (),
+    (),
+    (),
+    (),
+    (),
+    ((3, 0), (4, 0),),
+    ((5, 0),),
+    (),
+    (),
+    (),
+    (),
+    ((0, 1), (6, 0), (7, 0), (2, 1), (1, 1), (3, 1), (8, 0), (4, 1), (0, 2), (9, 0), (7, 1), (5, 1), (11, 0), (2, 2), (1, 2), (8, 1), (3, 2), (4, 2), (10, 0), (9, 1), (12, 0), (5, 2), (7, 2), (1, 3), (6, 1), (10, 1), (9, 2), (12, 1), (5, 3), (7, 3), (11, 1), (6, 2), (2, 3), (10, 2), (9, 3), (8, 2), (12, 2), (3, 3), (11, 2), (6, 3), (10, 3), (12, 3), (12, 4), (11, 3),),
 )
 BITS = 4
 OUT_UNIT, IN_UNIT, ATTN_UNIT, QKV_UNIT, UNITS = 0, 4, 8, 9, 12
@@ -441,7 +442,8 @@
 
         hidden = r.hidden_one[...] + dot(r.active[0:width, :], w_out[...])
         r.hidden_two[...] = hidden
-        normed_upper, normed_lower = split(hidden * inverse_root(hidden) * r.gain_final[...][None])
+        inverse_final = inverse_root(hidden)
+        normed_upper, normed_lower = split(hidden * inverse_final * r.gain_final[...][None])
         member_low = member.astype(LOW)
         pooled = (dot(member_low, normed_upper) + dot(member_low, normed_lower)) * share
         pooled = pooled.astype(LOW).astype(FULL)
@@ -551,7 +553,7 @@
 
         hidden = r.hidden_two[...]
         hidden_grad, r.small[0, 2:3, 0:model] = norm_backward(
-            hidden, inverse_root(hidden), r.gain_final[...][None], final_grad
+            hidden, inverse_final, r.gain_final[...][None], final_grad
         )
         r.hidden_grad[...] = hidden_grad
         r.branch[...] = hidden_grad.astype(LOW)
@@ -561,22 +563,25 @@
         send_branch.start()
         r.branch_half[0:width, :] = r.branch[:, own_half]
 
-        r.proj_grad_half[...] = r.proj_grad[:, own_half].astype(LOW)
-        r.w_proj_whole[...] = dot_tn(r.pooled[...].astype(LOW), r.proj_grad_half[...])
-        if direct:
-            r.w_proj_grad[...] = r.w_proj_whole[pl.ds(pl.multiple_of(row * own_rows, 8), own_rows), :]
-            publish(r.w_proj_grad)
-
-        send_active.wait()
-        send_branch.wait()
         per_tile = model * rows // ff
         if direct:
             for half_step in range(2):
                 pair = jnp.bitwise_xor(coordinate[Z_PAIR], 1 - half_step)
+                spans = [pl.ds(pl.multiple_of((2 * half_z + pair) * model, model), model) for half_z in range(2)]
+                if half_step == 0:
+                    own_parts = [
+                        dot_tn(r.active[0:width, span], r.branch_half[0:width, :]) for span in spans
+                    ]
+                    send_active.wait()
+                    send_branch.wait()
 
                 def tile(half_z):
-                    columns = pl.ds(pl.multiple_of((2 * half_z + pair) * model, model), model)
-                    value = dot_tn(r.active[:, columns], r.branch_half[...])
+                    if half_step == 0:
+                        value = own_parts[half_z] + dot_tn(
+                            r.active[width : 2 * width, spans[half_z]], r.branch_half[width : 2 * width, :]
+                        )
+                    else:
+                        value = dot_tn(r.active[:, spans[half_z]], r.branch_half[...])
                     for unit in range(per_tile):
                         for spot in range(per_tile):
                             start = (spot * per_tile + unit) * own_rows
@@ -594,6 +599,8 @@
                         for copy in sends:
                             copy.start()
         else:
+            send_active.wait()
+            send_branch.wait()
 
             @tiles(ff, model)
             def _(index, columns):
@@ -754,6 +761,14 @@
             r.small[0, 0:8, model : model + buckets] = sums[0:8]
             r.small[0, 0:8, model + LANES : model + LANES + buckets] = sums[8:16]
             small_exchange(0).start()
+
+        @then
+        def _():
+            r.proj_grad_half[...] = r.proj_grad[:, own_half].astype(LOW)
+            r.w_proj_whole[...] = dot_tn(r.pooled[...].astype(LOW), r.proj_grad_half[...])
+            if direct:
+                r.w_proj_grad[...] = r.w_proj_whole[pl.ds(pl.multiple_of(row * own_rows, 8), own_rows), :]
+                publish(r.w_proj_grad)
 
         for index in range(len(pieces) + 1):
             if index:

time: 94.8 us -> 89.9 us (0.948)
  Pallas kernels: 93.2 us -> 87.8 us
    pallas_call x1, Pallas kernels: 89.9 us -> 84.6 us  [step(): pl.pallas_call(make_kernel(sizes, names, small_inputs), out_shape=[jax.Sh...]
where the time goes in v5:
time: 89.9 us; the launch traced here: 89.3 us
  Pallas kernels  87.8 us (98%)
  between operations  1.48 us (2%)
    pallas_call x1, Pallas kernels, step(): pl.pallas_call(make_kernel(sizes, names, small_inputs), out_shape=[jax.Sh...  84.6 us
    pallas_call x1, Pallas kernels, step(): pl.pallas_call(copy_out, out_shape=[jax.ShapeDtypeStruct(shape, kind) for...  3.24 us

profile of v5, /device:TPU:0, one launch (start us, length us, event | category | flops | bytes accessed | tf_op | source)
XLA Modules:
  0.0 89.3 jit_solution(15997045652448680754)
XLA Ops:
  1.3 84.6 %shard_map.238 = (f32[1,1]{1,0:T(1,128)}, f32[256,768]{1,0:T(8,128)}, f32[768]{0:T(1024)}, f32[768]{0:T(1024)}, f32[768]{0:T(1024)}, /*index=5*/f32[12,32]{1,0:T...) custom-call(bf16[256,768]{1,0:T(8,128)(2,1)} %bitcast.7, ...), custom_call_target="tpu_custom_call" | custom-call | tf_op jit(solution)/shard_map/pallas_call | solution.py:961
  85.9 3.2 %shard_map.239 = (f32[1,1]{1,0:T(1,128)}, f32[256,768]{1,0:T(8,128)}, f32[768]{0:T(1024)}, f32[768]{0:T(1024)}, f32[768]{0:T(1024)}, /*index=5*/f32[12,32]{1,0:T...) custom-call(f32[1,1]{1,0:T(1,128)} %get-tuple-element.36.args_0_, ...), custom_call_target="tpu_custom_call" | custom-call | tf_op jit(solution)/shard_map/pallas_call | solution.py:976

commit v6 on v5

--- a/solution.py
+++ b/solution.py
@@ -18,20 +18,21 @@
 LANES = 128
 TILE = 512
 VMEM_LIMIT = 60 * 2**20
+WIDER_VMEM_LIMIT = 62 * 2**20
 
 Z_HALF, Z_PAIR, Y, X = range(4)
 ORDERS = (
     ((X,), (Y,), (Z_PAIR, Z_HALF)),
+    ((X,), (Y,), (Z_PAIR, Z_HALF)),
+    ((Z_PAIR,), (Y,), (X,), (Z_HALF,)),
     ((Y,), (X,), (Z_PAIR,), (Z_HALF,)),
-    ((Z_PAIR,), (Y,), (Z_HALF,), (X,)),
-    ((Z_PAIR,), (Y,), (Z_HALF,), (X,)),
-    ((X,), (Y,), (Z_PAIR, Z_HALF)),
     ((Y,), (X,), (Z_PAIR,), (Z_HALF,)),
+    ((Z_PAIR,), (X,), (Z_HALF,), (Y,)),
+    ((X,), (Y,), (Z_PAIR,), (Z_HALF,)),
     ((Z_PAIR,), (X,), (Y,), (Z_HALF,)),
-    ((X,), (Z_PAIR,), (Y,), (Z_HALF,)),
-    ((Z_PAIR,), (Y,), (X, Z_HALF)),
+    ((Z_PAIR,), (X,), (Y,), (Z_HALF,)),
     ((X,), (Y,), (Z_PAIR,), (Z_HALF,)),
-    ((X,), (Y,), (Z_PAIR,), (Z_HALF,)),
+    ((Y,), (Z_PAIR,), (X, Z_HALF)),
     ((Y,), (X,), (Z_PAIR,), (Z_HALF,)),
 )
 PLAN = (
@@ -46,23 +47,23 @@
     (),
     (),
     (),
-    (),
-    ((0, 0), (1, 0), (2, 0),),
-    (),
-    (),
-    (),
-    (),
-    (),
-    (),
-    (),
-    (),
-    ((3, 0), (4, 0),),
-    ((5, 0),),
-    (),
-    (),
-    (),
-    (),
-    ((0, 1), (6, 0), (7, 0), (2, 1), (1, 1), (3, 1), (8, 0), (4, 1), (0, 2), (9, 0), (7, 1), (5, 1), (11, 0), (2, 2), (1, 2), (8, 1), (3, 2), (4, 2), (10, 0), (9, 1), (12, 0), (5, 2), (7, 2), (1, 3), (6, 1), (10, 1), (9, 2), (12, 1), (5, 3), (7, 3), (11, 1), (6, 2), (2, 3), (10, 2), (9, 3), (8, 2), (12, 2), (3, 3), (11, 2), (6, 3), (10, 3), (12, 3), (12, 4), (11, 3),),
+    ((2, 0), (3, 0),),
+    (),
+    (),
+    (),
+    (),
+    ((0, 0),),
+    (),
+    (),
+    (),
+    (),
+    ((1, 0), (4, 0), (5, 0),),
+    (),
+    (),
+    (),
+    ((2, 1),),
+    (),
+    ((6, 0), (0, 1), (7, 0), (3, 1), (1, 1), (4, 1), (8, 0), (5, 1), (0, 2), (10, 0), (3, 2), (1, 2), (9, 0), (4, 2), (11, 0), (2, 2), (12, 0), (5, 2), (6, 1), (10, 1), (7, 1), (3, 3), (4, 3), (9, 1), (2, 3), (12, 1), (8, 1), (5, 3), (6, 2), (7, 2), (11, 1), (8, 2), (9, 2), (12, 2), (10, 2), (6, 3), (7, 3), (11, 2), (8, 3), (9, 3), (12, 3), (12, 4), (11, 3),),
 )
 BITS = 4
 OUT_UNIT, IN_UNIT, ATTN_UNIT, QKV_UNIT, UNITS = 0, 4, 8, 9, 12
@@ -117,9 +118,11 @@
     head_size = model // heads
     half = model // 2
     ff_half = ff // 2
+    assert heads * buckets <= half
     queries = rows * per_row
     parts = model // LANES
-    query_message = parts * per_row
+    query_message = -(-parts * per_row // 16) * 16
+    doc_message = 16
     row_bits = rows.bit_length() - 1
     direct = in_kernel_sums(rows, model)
 
@@ -364,7 +367,11 @@
             return carry
 
         lax.fori_loop(0, heads, spread_bias, 0)
-        r.small[0] = jnp.zeros((8, model + 2 * LANES), FULL)
+        r.small[0] = jnp.zeros((8, half), FULL)
+
+        def note_gain(which, gain_grad):
+            r.small[0, 2 * which : 2 * which + 1, :] = gain_grad[:, 0:half]
+            r.small[0, 2 * which + 1 : 2 * which + 2, :] = gain_grad[:, half:]
         r.diagonals[...] = jnp.zeros_like(r.diagonals)
 
         inputs = r.tokens[...].astype(FULL)
@@ -448,8 +455,9 @@
         pooled = (dot(member_low, normed_upper) + dot(member_low, normed_lower)) * share
         pooled = pooled.astype(LOW).astype(FULL)
 
-        own_queries = r.pooled_queries.at[pl.ds(pl.multiple_of(row * query_message, 8), query_message)]
-        own_doc = r.pooled_docs.at[pl.ds(pl.multiple_of(row * 8, 8), 8)]
+        own_queries = r.pooled_queries.at[pl.ds(pl.multiple_of(row * query_message, 16), query_message)]
+        own_doc = r.pooled_docs.at[pl.ds(pl.multiple_of(row * doc_message, 16), doc_message)]
+        r.stage[...] = jnp.zeros_like(r.stage)
 
         def spread(block, whole):
             for index in range(1, rows):
@@ -472,10 +480,10 @@
         @pl.when(is_query)
         def _():
             for part in range(parts):
-                spot = pl.multiple_of(row * query_message, 8) + part * per_row
-                r.pooled_queries[pl.ds(spot, per_row), :] = pooled[
+                r.stage[part * per_row : (part + 1) * per_row, :] = pooled[
                     0:per_row, part * LANES : (part + 1) * LANES
                 ]
+            own_queries[...] = r.stage[...].astype(LOW)
             spread(own_queries, r.pooled_queries)
             relay_queries.start()
             relay_docs.wait_recv()
@@ -483,22 +491,24 @@
 
         @pl.when(jnp.logical_not(is_query))
         def _():
-            own_doc[...] = jnp.zeros((8, LANES), FULL)
             for part in range(parts):
-                spot = pl.multiple_of(row * 8, 8) + part
-                r.pooled_docs[pl.ds(spot, 1), :] = pooled[0:1, part * LANES : (part + 1) * LANES]
+                r.stage[part : part + 1, :] = pooled[0:1, part * LANES : (part + 1) * LANES]
+            own_doc[...] = r.stage[0:doc_message, :].astype(LOW)
             spread(own_doc, r.pooled_docs)
             relay_docs.start()
             relay_queries.wait_recv()
             relay_docs.wait_send()
 
+        r.queries_wide[...] = r.pooled_queries[...].astype(FULL)
+        r.docs_wide[...] = r.pooled_docs[...].astype(FULL)
+
         for part in range(parts):
             lanes = slice(part * LANES, (part + 1) * LANES)
             for query in range(per_row):
-                r.pooled[query * rows : (query + 1) * rows, lanes] = r.pooled_queries[
+                r.pooled[query * rows : (query + 1) * rows, lanes] = r.queries_wide[
                     pl.ds(part * per_row + query, rows, stride=query_message), :
                 ]
-            r.pooled[queries:, lanes] = r.pooled_docs[pl.ds(part, rows, stride=8), :]
+            r.pooled[queries:, lanes] = r.docs_wide[pl.ds(part, rows, stride=doc_message), :]
 
         loaded(5)
         w_proj = r.w_proj_here
@@ -552,9 +562,10 @@
             final_grad = jnp.where(seg_column == query, pooled_grad[query : query + 1, :], final_grad)
 
         hidden = r.hidden_two[...]
-        hidden_grad, r.small[0, 2:3, 0:model] = norm_backward(
+        hidden_grad, gain_grad = norm_backward(
             hidden, inverse_final, r.gain_final[...][None], final_grad
         )
+        note_gain(2, gain_grad)
         r.hidden_grad[...] = hidden_grad
         r.branch[...] = hidden_grad.astype(LOW)
         own_half = pl.ds(pl.multiple_of(tower * half, LANES), half)
@@ -638,9 +649,10 @@
         @then
         def _():
             hidden = r.hidden_one[...]
-            through, r.small[0, 1:2, 0:model] = norm_backward(
+            through, gain_grad = norm_backward(
                 hidden, inverse_root(hidden), r.gain_ff[...][None], r.normed_grad[...]
             )
+            note_gain(1, gain_grad)
             hidden_grad = r.hidden_grad[...] + through
             r.hidden_grad[...] = hidden_grad
             r.attn[...] = hidden_grad.astype(LOW)
@@ -745,9 +757,10 @@
         @then
         def _():
             inputs = r.tokens[...].astype(FULL)
-            through, r.small[0, 0:1, 0:model] = norm_backward(
+            through, gain_grad = norm_backward(
                 inputs, inverse_root(inputs), r.gain_attn[...][None], r.normed_grad[...]
             )
+            note_gain(0, gain_grad)
             r.tokens_grad[...] = r.hidden_grad[...] + through
             publish(r.tokens_grad)
 
@@ -758,8 +771,8 @@
             offset_upper, offset_lower = split(offsets)
             hot_low = r.hot[...]
             sums = dot_nt(offset_upper, hot_low) + dot_nt(offset_lower, hot_low)
-            r.small[0, 0:8, model : model + buckets] = sums[0:8]
-            r.small[0, 0:8, model + LANES : model + LANES + buckets] = sums[8:16]
+            for head in range(heads):
+                r.small[0, 6:7, head * buckets : (head + 1) * buckets] = sums[head : head + 1]
             small_exchange(0).start()
 
         @then
@@ -781,11 +794,11 @@
             for step in range(row_bits + 1):
                 small_finish(step)
         total = row_bits + 1
-        r.gain_attn_grad[...] = r.small[total, 0, 0:model]
-        r.gain_ff_grad[...] = r.small[total, 1, 0:model]
-        r.gain_final_grad[...] = r.small[total, 2, 0:model]
-        r.rel_bias_grad[0:8, :] = r.small[total, 0:8, model : model + buckets]
-        r.rel_bias_grad[8:heads, :] = r.small[total, 0 : heads - 8, model + LANES : model + LANES + buckets]
+        for which, result in enumerate((r.gain_attn_grad, r.gain_ff_grad, r.gain_final_grad)):
+            result[0:half] = r.small[total, 2 * which]
+            result[half:model] = r.small[total, 2 * which + 1]
+        for head in range(heads):
+            r.rel_bias_grad[head : head + 1, :] = r.small[total, 6:7, head * buckets : (head + 1) * buckets]
         for result in (r.gain_attn_grad, r.gain_ff_grad, r.gain_final_grad, r.rel_bias_grad):
             publish(result)
         if direct:
@@ -842,6 +855,7 @@
         per_row = positives.shape[1]
         half = model // 2
         wide = 2 * width
+        query_message = -(-per_row * model // LANES // 16) * 16
         queries = rows * per_row
         row_bits = rows.bit_length() - 1
         own_rows = model // rows
@@ -919,8 +933,11 @@
             active=((2 * width, ff), LOW),
             inner=((width, ff), FULL),
             hidden_two=((width, model), FULL),
-            pooled_queries=((rows * per_row * model // LANES, LANES), FULL),
-            pooled_docs=((rows * 8, LANES), FULL),
+            pooled_queries=((rows * query_message, LANES), LOW),
+            pooled_docs=((rows * 16, LANES), LOW),
+            queries_wide=((rows * query_message, LANES), FULL),
+            docs_wide=((rows * 16, LANES), FULL),
+            stage=((query_message, LANES), FULL),
             pooled=((queries + rows, model), FULL),
             proj_grad=((queries + rows, model), FULL),
             proj_grad_half=((queries + rows, half), LOW),
@@ -939,8 +956,8 @@
             queries_turned=((model, width), LOW),
             qkv_grad=((width, 3 * model), LOW),
             qkv_half=((2 * width, model + half), LOW),
-            small=((row_bits + 2, 8, model + 2 * LANES), FULL),
-            small_in=((row_bits + 1, 8, model + 2 * LANES), FULL),
+            small=((row_bits + 2, 8, half), FULL),
+            small_in=((row_bits + 1, 8, half), FULL),
         )
         scratch.update(held)
         semaphores = dict(
@@ -969,7 +986,9 @@
             + nears
             + arrived,
             compiler_params=pltpu.CompilerParams(
-                collective_id=0, has_side_effects=True, vmem_limit_bytes=VMEM_LIMIT
+                collective_id=0,
+                has_side_effects=True,
+                vmem_limit_bytes=VMEM_LIMIT if direct else WIDER_VMEM_LIMIT,
             ),
         )(*[array for array, _ in inputs.values()])
         if direct:

time: 89.9 us -> 87.8 us (0.977)
  Pallas kernels: 87.8 us -> 86 us
    pallas_call x1, Pallas kernels: 84.6 us -> 82.7 us  [step(): pl.pallas_call(make_kernel(sizes, names, small_inputs), out_shape=[jax.Sh...]
where the time goes in v6:
time: 87.8 us; the launch traced here: 87.5 us
  Pallas kernels  86 us (98%)
  between operations  1.48 us (2%)
    pallas_call x1, Pallas kernels, step(): pl.pallas_call(make_kernel(sizes, names, small_inputs), out_shape=[jax.Sh...  82.7 us
    pallas_call x1, Pallas kernels, step(): pl.pallas_call(copy_out, out_shape=[jax.ShapeDtypeStruct(shape, kind) for...  3.24 us

profile of v6, /device:TPU:0, one launch (start us, length us, event | category | flops | bytes accessed | tf_op | source)
XLA Modules:
  0.0 87.5 jit_solution(11787611449792007304)
XLA Ops:
  1.3 82.7 %shard_map.238 = (f32[1,1]{1,0:T(1,128)}, f32[256,768]{1,0:T(8,128)}, f32[768]{0:T(1024)}, f32[768]{0:T(1024)}, f32[768]{0:T(1024)}, /*index=5*/f32[12,32]{1,0:T...) custom-call(bf16[256,768]{1,0:T(8,128)(2,1)} %bitcast.7, ...), custom_call_target="tpu_custom_call" | custom-call | tf_op jit(solution)/shard_map/pallas_call | solution.py:978
  84.1 3.2 %shard_map.239 = (f32[1,1]{1,0:T(1,128)}, f32[256,768]{1,0:T(8,128)}, f32[768]{0:T(1024)}, f32[768]{0:T(1024)}, f32[768]{0:T(1024)}, /*index=5*/f32[12,32]{1,0:T...) custom-call(f32[1,1]{1,0:T(1,128)} %get-tuple-element.36.args_0_, ...), custom_call_target="tpu_custom_call" | custom-call | tf_op jit(solution)/shard_map/pallas_call | solution.py:995

commit v7 on v6

--- a/solution.py
+++ b/solution.py
@@ -227,8 +227,13 @@
             if len(ORDERS[unit][step]) > 1:
                 into = into.at[code - 1]
             elif half is not None:
-                place[Z_PAIR] = jnp.bitwise_xor(coordinate[Z_PAIR], 1 - half)
-                into = into.at[:, place[Z_PAIR]]
+                pair_step, half_z = half
+                place[Z_HALF] = half_z
+                if Z_PAIR in ORDERS[unit][step]:
+                    into = into.at[half_z]
+                else:
+                    place[Z_PAIR] = jnp.bitwise_xor(coordinate[Z_PAIR], 1 - pair_step)
+                    into = into.at[half_z, place[Z_PAIR]]
             peer = row
             for spot, bit in enumerate(ORDERS[unit][step]):
                 peer = jnp.bitwise_xor(peer, ((code >> spot) & 1) << (3 - bit))
@@ -243,8 +248,9 @@
 
         def exchanges(unit, step):
             bits = ORDERS[unit][step]
-            if step == 0 and unit < IN_UNIT and bits[0] in (X, Y) and len(bits) == 1:
-                return [exchange(unit, step, 1, half) for half in range(2)]
+            if step == 0 and unit < IN_UNIT and bits in ((X,), (Y,), (Z_PAIR,)):
+                pair_steps = range(1 if Z_PAIR in bits else 2)
+                return [exchange(unit, step, 1, (pair, half_z)) for pair in pair_steps for half_z in range(2)]
             return [exchange(unit, step, code) for code in range(1, 2 ** len(bits))]
 
         def all_of(ref, send_sem, recv_sem):
@@ -602,13 +608,15 @@
 
                 for half_z in range(2):
                     tile(half_z)
-                for unit in range(OUT_UNIT, IN_UNIT):
-                    sends = exchanges(unit, 0)
-                    if len(sends) == 2:
-                        sends[half_step].start()
-                    elif half_step == (Z_PAIR not in ORDERS[unit][0]):
-                        for copy in sends:
-                            copy.start()
+                    for unit in range(OUT_UNIT, IN_UNIT):
+                        sends = exchanges(unit, 0)
+                        at = 2 * half_step + half_z
+                        if len(ORDERS[unit][0]) == 1:
+                            if at < len(sends):
+                                sends[at].start()
+                        elif at == 3:
+                            for copy in sends:
+                                copy.start()
         else:
             send_active.wait()
             send_branch.wait()

time: 87.8 us -> 88.1 us (level)
  no operation moved by 1% of the time
where the time goes in v7:
time: 88.1 us; the launch traced here: 87.6 us
  Pallas kernels  86.1 us (98%)
  between operations  1.48 us (2%)
    pallas_call x1, Pallas kernels, step(): pl.pallas_call(make_kernel(sizes, names, small_inputs), out_shape=[jax.Sh...  82.9 us
    pallas_call x1, Pallas kernels, step(): pl.pallas_call(copy_out, out_shape=[jax.ShapeDtypeStruct(shape, kind) for...  3.24 us

profile of v7, /device:TPU:0, one launch (start us, length us, event | category | flops | bytes accessed | tf_op | source)
XLA Modules:
  0.0 87.6 jit_solution(3436618551637945366)
XLA Ops:
  1.3 82.9 %shard_map.238 = (f32[1,1]{1,0:T(1,128)}, f32[256,768]{1,0:T(8,128)}, f32[768]{0:T(1024)}, f32[768]{0:T(1024)}, f32[768]{0:T(1024)}, /*index=5*/f32[12,32]{1,0:T...) custom-call(bf16[256,768]{1,0:T(8,128)(2,1)} %bitcast.7, ...), custom_call_target="tpu_custom_call" | custom-call | tf_op jit(solution)/shard_map/pallas_call | solution.py:986
  84.2 3.2 %shard_map.239 = (f32[1,1]{1,0:T(1,128)}, f32[256,768]{1,0:T(8,128)}, f32[768]{0:T(1024)}, f32[768]{0:T(1024)}, f32[768]{0:T(1024)}, /*index=5*/f32[12,32]{1,0:T...) custom-call(f32[1,1]{1,0:T(1,128)} %get-tuple-element.36.args_0_, ...), custom_call_target="tpu_custom_call" | custom-call | tf_op jit(solution)/shard_map/pallas_call | solution.py:1003
